TPU v7x, 32 devices: a whole 2x2x4 slice. The times are simulated.
32 devices in a mesh: groups: 2 (over y), expert: 8 (over z, x), head: 2 (over core).
Axes of the slice: x: 2, y: 2, z: 4, core: 2. Of those that a mesh axis runs over, the one named last changes fastest.
Arguments:
- moe_in: bfloat16 [128, 7168], P(('groups', 'expert'), 'head'), parts along dimension 0, may hold values from -6 to 6
- routes: int32 [128, 2], P(('groups', 'expert')), parts along dimension 0, may hold values from 0 to 7, all different within a row; in each aligned block of 8 rows (0 to 7, 8 to 15, ...) at most 2 rows name the same one
- gate_weights: float32 [128, 2], P(('groups', 'expert')), parts along dimension 0, may hold values from 0.1 to 1
- w_gate: bfloat16 [7168, 16384], P('head', 'expert'), may hold values from -0.0625 to 0.0625
- w_up: bfloat16 [7168, 16384], P('head', 'expert'), may hold values from -0.0625 to 0.0625
- w_down: bfloat16 [16384, 7168], P('expert', 'head'), may hold values from -0.125 to 0.125
Outputs:
- moe_out: bfloat16 [128, 7168], P(('groups', 'expert'), 'head'), parts along dimension 0
There are 2 independent parts, one for each index of `groups`. A program takes and returns all parts, laid end to end along the dimension named above; an argument that names none is the same for every part. Nothing has to cross between parts.
Inputs may be any that keep to these rules, and one draw needn't show every extreme that they name: `routes`: each row names 2 different experts; among the 8 rows of one device no expert is named more than 2 times, a bound that some block reaches.
All inputs are finite; a program needn't handle non-finite values.
Results may differ from a plain program's by a relative error of at most 0.0058.
Values may be sent and summed in bfloat16 or wider, within the bound.
No kernel may reach another device: no remote copies, remote signals or barrier semaphores. Data moves between devices by JAX's collectives and lax.ppermute only.
A program may use at most 128 MiB of HBM per device.

v0:
```python
import jax
import jax.numpy as jnp
from jax import lax
from jax.sharding import PartitionSpec as P

FLIGHT = 8
CAP = 2


def per_device(moe_in, routes, gate_weights, w_gate, w_up, w_down):
    expert_ids = jnp.arange(FLIGHT, dtype=jnp.int32)
    matched = (routes[:, :, None] == expert_ids[None, None, :]).astype(jnp.float32)
    chosen = jnp.sum(matched, axis=1)
    gate_hit = jnp.sum(matched * gate_weights[:, :, None], axis=1)
    slot_index = jnp.cumsum(chosen, axis=0) - chosen
    slot_ids = jnp.arange(CAP, dtype=jnp.float32)
    placing = chosen[:, :, None] * (slot_index[:, :, None] == slot_ids[None, None, :]).astype(
        jnp.float32
    )
    packed_rows = jnp.einsum(
        "rfc,rd->fcd", placing.astype(jnp.bfloat16), moe_in, preferred_element_type=jnp.float32
    ).astype(jnp.bfloat16)
    copies = lax.axis_size("expert") // FLIGHT
    width = moe_in.shape[1]
    outgoing = jnp.broadcast_to(packed_rows[:, None], (FLIGHT, copies, CAP, width)).reshape(
        FLIGHT * copies, CAP, width
    )
    arrived = lax.all_to_all(outgoing, "expert", split_axis=0, concat_axis=0, tiled=True)
    sources, count, features = arrived.shape
    arrived_rows = arrived.reshape(sources * count, features)
    gate_part = jnp.dot(arrived_rows, w_gate, preferred_element_type=jnp.float32)
    up_part = jnp.dot(arrived_rows, w_up, preferred_element_type=jnp.float32)
    gate_pre, up_pre = lax.psum((gate_part, up_part), "head")
    hidden = (jax.nn.silu(gate_pre) * up_pre).astype(jnp.bfloat16)
    partial_out = jnp.dot(hidden, w_down, preferred_element_type=jnp.float32).astype(jnp.bfloat16)
    returned = lax.all_to_all(
        partial_out.reshape(sources, count, features),
        "expert",
        split_axis=0,
        concat_axis=0,
        tiled=True,
    )
    summed = jnp.sum(returned.reshape(FLIGHT, copies, CAP, width).astype(jnp.float32), axis=1)
    spread = placing * gate_hit[:, :, None]
    moe_out = jnp.einsum("rfc,fcd->rd", spread, summed, precision=lax.Precision.HIGHEST).astype(
        jnp.bfloat16
    )
    return moe_out


def solution(mesh):
    in_specs = (
        P(("groups", "expert"), "head"),
        P(("groups", "expert"), None),
        P(("groups", "expert"), None),
        P("head", "expert"),
        P("head", "expert"),
        P("expert", "head"),
    )
    out_specs = P(("groups", "expert"), "head")
    return jax.shard_map(
        per_device, mesh=mesh, in_specs=in_specs, out_specs=out_specs, check_vma=False
    )
```

profile of v0, /device:TPU:0, one launch (start us, length us, event | category | flops | bytes accessed | tf_op | source)
XLA Modules:
  0.0 78.3 jit_solution(68433312828106457)
XLA Ops:
  6.5 0.0 copy-start
  6.5 0.0 all-reduce.3.cloned.1.call-start
  6.5 0.8 %select_reduce_fusion = (f32[8,8]{1,0:T(8,128)S(1)}, f32[8,8]{1,0:T(8,128)S(1)}) fusion(f32[8,2]{0,1:T(2,128)} %param.8, s32[8,2]{0,1:T(2,128)} %param.7), kind=kLoop, calls=%fused_computation.10 | loop fusion | flops 512 | bytes 640 | tf_op jit(solution)/shard_map/reduce_sum | solution.py:14
  7.4 0.0 copy-done
  7.4 0.2 convolution_convert_fusion.1
  7.6 0.1 copy.22
  7.7 14.3 %all_to_all.10 = bf16[8,2,3584]{2,1,0:T(2,128)(2,1)S(1)} all-to-all(bf16[8,2,3584]{2,1,0:T(2,128)(2,1)S(1)} %copy.22), channel_id=1, replica_groups=mesh['groups'=2,'expert'=8,'head'=2] {'expert'}, dimensions={0} | all-to-all | bytes 229376 | tf_op jit(solution)/shard_map/all_to_all | solution.py:28
  22.0 0.0 copy-start.1
  22.1 8.0 %fusion.15 = f32[16,2048]{1,0:T(8,128)} fusion(bf16[16,3584]{1,0:T(8,128)(2,1)S(1)} %reshape.22, bf16[3584,2048]{1,0:T(8,128)(2,1)} %param.10), kind=kOutput, calls=%fused_computation.25 | convolution fusion | flops 234881024 | bytes 14925824 | tf_op jit(solution)/shard_map/dot_general | solution.py:32
  30.0 1.4 %copy-done.1 = bf16[3584,2048]{1,0:T(8,128)(2,1)S(1)} copy-done((bf16[3584,2048]{1,0:T(8,128)(2,1)S(1)}, bf16[3584,2048]{1,0:T(8,128)(2,1)}, u32[]{:S(2)}) %copy-start.1) | copy-done | bytes 14680088
  31.4 2.7 %fusion.14 = f32[16,2048]{1,0:T(8,128)} fusion(bf16[16,3584]{1,0:T(8,128)(2,1)S(1)} %reshape.22, bf16[3584,2048]{1,0:T(8,128)(2,1)S(1)} %copy-done.1), kind=kOutput, calls=%fused_computation.24 | convolution fusion | flops 234881024 | bytes 14925824 | tf_op jit(solution)/shard_map/dot_general | solution.py:31
  34.1 0.0 all-reduce.3.cloned.1.call-update
  34.1 16.2 %all-reduce.3.cloned.1.call-done = (f32[16,2048]{1,0:T(8,128)}, f32[16,2048]{1,0:T(8,128)}) async-done(((f32[16,2048]{1,0:T(8,128)}, f32[16,2048]{1,0:T(8,128)}), (f32[16,2048]{1,0:T(8,128)}, f32[16,2048]{1,0:T(8,128)})) %all-reduce.3.cloned.1.call-update) | async-done | bytes 262160 | tf_op jit(solution)/shard_map/psum | solution.py:33
  50.3 7.3 %convolution_convert_fusion = bf16[16,3584]{1,0:T(8,128)(2,1)S(1)} fusion(bf16[2048,3584]{1,0:T(8,128)(2,1)} %param.11, f32[16,2048]{1,0:T(8,128)} %get-tuple-element.7, f32[16,2048]{1,0:T(8,128)} %get-tuple-element.8), kind=kOutput, calls=%fused_computation | convolution fusion | flops 235134976 | bytes 15056896 | tf_op jit(solution)/shard_map/dot_general | solution.py:35
  57.7 0.1 reshape.23
  57.7 12.8 %all_to_all.11 = bf16[8,2,3584]{2,1,0:T(2,128)(2,1)S(1)} all-to-all(bf16[8,2,3584]{2,1,0:T(2,128)(2,1)S(1)} %reshape.23), channel_id=1, replica_groups=mesh['groups'=2,'expert'=8,'head'=2] {'expert'}, dimensions={0} | all-to-all | bytes 229376 | tf_op jit(solution)/shard_map/all_to_all | solution.py:36
  70.5 0.9 %fusion = bf16[8,3584]{1,0:T(8,128)(2,1)} fusion(bf16[8,2,3584]{2,1,0:T(2,128)(2,1)S(1)} %all_to_all.11, f32[8,8]{1,0:T(8,128)S(1)} %get-tuple-element.5, f32[8,8]{1,0:T(8,128)S(1)} %get-tuple-element.6, f32[8,8]{1,0:T(8,128)S(1)} %sub.7), kind=kOutput, calls=%fused_computation.3 | convolution fusion | flops 5534080 | bytes 172800 | tf_op jit(solution)/shard_map/rfc,fcd->rd/dot_general | solution.py:45
  (3 shorter events, 0.1 us)
Async XLA Ops:
  6.5 0.9 %copy-start = (bf16[8,3584]{1,0:T(8,128)(2,1)S(1)}, bf16[8,3584]{1,0:T(8,128)(2,1)}, u32[]{:S(2)}) copy-start(bf16[8,3584]{1,0:T(8,128)(2,1)} %param.6) | copy-start | bytes 172036
  6.5 43.8 %all-reduce.3.cloned.1.call-start = ((), (), s32[]{:S(2)}) async-start(), calls=%async_computation.2 | async-start | bytes 524288 | tf_op jit(solution)/shard_map/psum | solution.py:33
  22.0 9.4 %copy-start.1 = (bf16[3584,2048]{1,0:T(8,128)(2,1)S(1)}, bf16[3584,2048]{1,0:T(8,128)(2,1)}, u32[]{:S(2)}) copy-start(bf16[3584,2048]{1,0:T(8,128)(2,1)} %param.9) | copy-start | bytes 44040196
Sparse Core Ops, SparseCore 0:
  34.2 16.0 all-reduce.2
where the time goes:
time: 78.5 us; the launch traced here: 78.3 us
  blocking collectives  27.1 us (35%)
  matrix products  19.1 us (24%)
  waiting for transfers between devices  16.2 us (21%)
  between operations  13.4 us (17%)
  local copies, waits for them, and re-layouts  1.63 us (2%)
  other arithmetic  0.82 us (1%)
    psum x1, waiting for transfers between devices, per_device(): gate_pre, up_pre = lax.psum((gate_part, up_part), 'head')  16.2 us
    all_to_all x1, blocking collectives, per_device(): lax.all_to_all(outgoing, 'expert', split_axis=0, concat_axis=0, tiled=True)  14.3 us
    all_to_all x1, blocking collectives, per_device(): lax.all_to_all(partial_out.reshape(sources, count, features), 'expert', s...  12.8 us
    dot_general x1, matrix products, per_device(): up_part = jnp.dot(arrived_rows, w_up, preferred_element_type=jnp.float32)  7.99 us
    dot_general x1, matrix products, per_device(): jnp.dot(hidden, w_down, preferred_element_type=jnp.float32)  7.33 us
    dot_general x1, matrix products, per_device(): jnp.dot(arrived_rows, w_gate, preferred_element_type=jnp.float32)  2.66 us
  transfers between devices with their start and end apart: 1, of which 1 were waited for; matrix products, arithmetic and copies ran while one was open for 0% of the time, Pallas kernels for 0%

commit v1 on v0

--- a/solution.py
+++ b/solution.py
@@ -30,7 +30,10 @@
     arrived_rows = arrived.reshape(sources * count, features)
     gate_part = jnp.dot(arrived_rows, w_gate, preferred_element_type=jnp.float32)
     up_part = jnp.dot(arrived_rows, w_up, preferred_element_type=jnp.float32)
-    gate_pre, up_pre = lax.psum((gate_part, up_part), "head")
+    cores = lax.axis_size("head")
+    swap = [(i, (i + 1) % cores) for i in range(cores)]
+    gate_pre = gate_part + lax.ppermute(gate_part, "head", swap)
+    up_pre = up_part + lax.ppermute(up_part, "head", swap)
     hidden = (jax.nn.silu(gate_pre) * up_pre).astype(jnp.bfloat16)
     partial_out = jnp.dot(hidden, w_down, preferred_element_type=jnp.float32).astype(jnp.bfloat16)
     returned = lax.all_to_all(

time: 78.5 us -> 42.1 us (0.54)
  waiting for transfers between devices: 16.2 us -> 1.02 us
  between operations: 13.4 us -> 0.06 us
  matrix products: 19.1 us -> 12.4 us
  blocking collectives: 27.1 us -> 23.9 us
  local copies, waits for them, and re-layouts: 1.63 us -> 3.11 us
    psum x1 -> x0, waiting for transfers between devices: 16.2 us -> none  [per_device(): gate_pre, up_pre = lax.psum((gate_part, up_part), 'head')]
    dot_general x1, matrix products: 7.33 us -> 2 us  [per_device(): jnp.dot(hidden, w_down, preferred_element_type=jnp.float32)]
    all_to_all x1, blocking collectives: 12.8 us -> 9.62 us  [per_device(): lax.all_to_all(partial_out.reshape(sources, count, features), 'expert', s...]
    unnamed x4 -> x12, local copies, waits for them, and re-layouts: 1.43 us -> 2.91 us
    ppermute x0 -> x2, waiting for transfers between devices: none -> 1.02 us  [the longest x1 0.84 us: per_device(): gate_pre = gate_part + lax.ppermute(gate_part, 'head', swap)]
  transfers between devices with their start and end apart: 1 -> 2, of which waited for: 1 -> 2; matrix products, arithmetic and copies ran while one was open for 0% -> 0% of each run, Pallas kernels for 0% -> 0%
where the time goes in v1:
time: 42.1 us; the launch traced here: 41.9 us
  blocking collectives  23.9 us (57%)
  matrix products  12.4 us (29%)
  local copies, waits for them, and re-layouts  3.11 us (7%)
  waiting for transfers between devices  1.02 us (2%)
  other arithmetic  0.81 us (2%)
  starting transfers between devices  0.52 us (1%)
    all_to_all x1, blocking collectives, per_device(): lax.all_to_all(outgoing, 'expert', split_axis=0, concat_axis=0, tiled=True)  14.3 us
    all_to_all x1, blocking collectives, per_device(): lax.all_to_all(partial_out.reshape(sources, count, features), 'expert', s...  9.62 us
    dot_general x1, matrix products, per_device(): up_part = jnp.dot(arrived_rows, w_up, preferred_element_type=jnp.float32)  7.33 us
    unnamed x12, local copies, waits for them, and re-layouts  2.91 us
    dot_general x1, matrix products, per_device(): jnp.dot(arrived_rows, w_gate, preferred_element_type=jnp.float32)  2 us
    dot_general x1, matrix products, per_device(): jnp.dot(hidden, w_down, preferred_element_type=jnp.float32)  2 us
    dot_general x1, matrix products, per_device(): jnp.einsum('rfc,fcd->rd', spread, summed, precision=lax.Precision.HIGHEST)  0.88 us
  transfers between devices with their start and end apart: 2, of which 2 were waited for; matrix products, arithmetic and copies ran while one was open for 0% of the time, Pallas kernels for 0%

profile of v1, /device:TPU:0, one launch (start us, length us, event | category | flops | bytes accessed | tf_op | source)
XLA Modules:
  0.0 41.9 jit_solution(5102902673220997026)
XLA Ops:
  0.0 0.0 copy-start
  0.0 0.8 %select_reduce_fusion = (f32[8,8]{1,0:T(8,128)S(1)}, f32[8,8]{1,0:T(8,128)S(1)}) fusion(f32[8,2]{0,1:T(2,128)} %param.8, s32[8,2]{0,1:T(2,128)} %param.7), kind=kLoop, calls=%fused_computation.10 | loop fusion | flops 512 | bytes 640 | tf_op jit(solution)/shard_map/reduce_sum | solution.py:14
  0.8 0.0 copy-done
  0.9 0.2 convolution_convert_fusion.1
  1.1 0.1 copy.22
  1.2 14.3 %all_to_all.10 = bf16[8,2,3584]{2,1,0:T(2,128)(2,1)S(1)} all-to-all(bf16[8,2,3584]{2,1,0:T(2,128)(2,1)S(1)} %copy.22), channel_id=1, replica_groups=mesh['groups'=2,'expert'=8,'head'=2] {'expert'}, dimensions={0} | all-to-all | bytes 229376 | tf_op jit(solution)/shard_map/all_to_all | solution.py:28
  15.5 0.0 copy-start.1
  15.5 0.0 slice-start
  15.5 0.0 slice-start.1
  15.5 7.3 %fusion.15 = f32[16,2048]{1,0:T(8,128)S(1)} fusion(bf16[16,3584]{1,0:T(8,128)(2,1)S(1)} %reshape.22, bf16[3584,2048]{1,0:T(8,128)(2,1)} %param.10), kind=kOutput, calls=%fused_computation.25 | convolution fusion | flops 234881024 | bytes 14925824 | tf_op jit(solution)/shard_map/dot_general | solution.py:32
  22.9 2.0 %copy-done.1 = bf16[3584,2048]{1,0:T(8,128)(2,1)S(1)} copy-done((bf16[3584,2048]{1,0:T(8,128)(2,1)S(1)}, bf16[3584,2048]{1,0:T(8,128)(2,1)}, u32[]{:S(2)}) %copy-start.1) | copy-done | bytes 14680088
  24.9 2.0 %fusion.14 = f32[16,2048]{1,0:T(8,128)S(1)} fusion(bf16[16,3584]{1,0:T(8,128)(2,1)S(1)} %reshape.22, bf16[3584,2048]{1,0:T(8,128)(2,1)S(1)} %copy-done.1), kind=kOutput, calls=%fused_computation.24 | convolution fusion | flops 234881024 | bytes 14925824 | tf_op jit(solution)/shard_map/dot_general | solution.py:31
  26.9 0.0 collective-permute-start
  26.9 0.5 %collective-permute-start.1 = (f32[16,2048]{1,0:T(8,128)S(1)}, f32[16,2048]{1,0:T(8,128)S(1)}, u32[]{:S(2)}, u32[]{:S(2)}) collective-permute-start(f32[16,2048]{1,0:T(8,128)S(1)} %fusion.15), channel_id=1, source_target_pairs={{0,1},{1,0},{2,3},{3,2},{4,5},{5,4},{6,7},{7,6},{8,9},{9,8},{10,11... | collective-permute-start | bytes 393224 | tf_op jit(solution)/shard_map/ppermute | solution.py:36
  27.4 0.8 %collective-permute-done = f32[16,2048]{1,0:T(8,128)S(1)} collective-permute-done((f32[16,2048]{1,0:T(8,128)S(1)}, f32[16,2048]{1,0:T(8,128)S(1)}, u32[]{:S(2)}, u32[]{:S(2)}) %collective-permute-start) | collective-permute-done | bytes 131104 | tf_op jit(solution)/shard_map/ppermute | solution.py:35
  28.2 0.2 collective-permute-done.1
  28.4 0.0 slice-done
  28.4 0.0 slice-done.1
  28.4 0.3 slice-done.2
  28.7 0.6 %slice-done.3 = s8[2097152]{0:T(1024)(128)(4,1)S(1)} async-done(((s8[14680064]{0:T(1024)(128)(4,1)}), s8[2097152]{0:T(1024)(128)(4,1)S(1)}, s32[]{:S(2)}) %slice-start.3) | async-done | bytes 2097176
  29.3 2.0 %convolution_convert_fusion = bf16[16,3584]{1,0:T(8,128)(2,1)S(1)} fusion(bf16[2048,3584]{1,0:T(8,128)(2,1)S(1)} %bitcast.13, f32[16,2048]{1,0:T(8,128)S(1)} %fusion.15, f32[16,2048]{1,0:T(8,128)S(1)} %collective-permute-done.1, f32[16,2048]{1,0:T(8,128)S(1)} %fusion.14, f32[16,2048]{1,0:T(8,128)S(1)} %collective-permute-done), kind=kOutput, calls=%fused_computation | convolution fusion | flops 235200512 | bytes 15319040 | tf_op jit(solution)/shard_map/dot_general | solution.py:38
  31.3 0.1 reshape.23
  31.4 9.6 %all_to_all.11 = bf16[8,2,3584]{2,1,0:T(2,128)(2,1)S(1)} all-to-all(bf16[8,2,3584]{2,1,0:T(2,128)(2,1)S(1)} %reshape.23), channel_id=1, replica_groups=mesh['groups'=2,'expert'=8,'head'=2] {'expert'}, dimensions={0} | all-to-all | bytes 229376 | tf_op jit(solution)/shard_map/all_to_all | solution.py:39
  41.0 0.9 %fusion = bf16[8,3584]{1,0:T(8,128)(2,1)} fusion(bf16[8,2,3584]{2,1,0:T(2,128)(2,1)S(1)} %all_to_all.11, f32[8,8]{1,0:T(8,128)S(1)} %get-tuple-element.5, f32[8,8]{1,0:T(8,128)S(1)} %get-tuple-element.6, f32[8,8]{1,0:T(8,128)S(1)} %sub.7), kind=kOutput, calls=%fused_computation.3 | convolution fusion | flops 5534080 | bytes 172800 | tf_op jit(solution)/shard_map/rfc,fcd->rd/dot_general | solution.py:48
  (6 shorter events, 0.1 us)
Async XLA Ops:
  0.0 0.9 %copy-start = (bf16[8,3584]{1,0:T(8,128)(2,1)S(1)}, bf16[8,3584]{1,0:T(8,128)(2,1)}, u32[]{:S(2)}) copy-start(bf16[8,3584]{1,0:T(8,128)(2,1)} %param.6) | copy-start | bytes 172036
  15.5 9.4 %copy-start.1 = (bf16[3584,2048]{1,0:T(8,128)(2,1)S(1)}, bf16[3584,2048]{1,0:T(8,128)(2,1)}, u32[]{:S(2)}) copy-start(bf16[3584,2048]{1,0:T(8,128)(2,1)} %param.9) | copy-start | bytes 44040196
  15.5 12.9 %slice-start = ((s8[14680064]{0:T(1024)(128)(4,1)}), s8[4194304]{0:T(1024)(128)(4,1)S(1)}, s32[]{:S(2)}) async-start(s8[14680064]{0:T(1024)(128)(4,1)} %bitcast.12), calls=%async_computation.2 | async-start | bytes 8388608
  15.5 12.9 %slice-start.1 = ((s8[14680064]{0:T(1024)(128)(4,1)}), s8[4194304]{0:T(1024)(128)(4,1)S(1)}, s32[]{:S(2)}) async-start(s8[14680064]{0:T(1024)(128)(4,1)} %bitcast.12), calls=%async_computation.3 | async-start | bytes 8388608
  24.9 3.8 %slice-start.2 = ((s8[14680064]{0:T(1024)(128)(4,1)}), s8[4194304]{0:T(1024)(128)(4,1)S(1)}, s32[]{:S(2)}) async-start(s8[14680064]{0:T(1024)(128)(4,1)} %bitcast.12), calls=%async_computation.4 | async-start | bytes 8388608
  24.9 4.4 %slice-start.3 = ((s8[14680064]{0:T(1024)(128)(4,1)}), s8[2097152]{0:T(1024)(128)(4,1)S(1)}, s32[]{:S(2)}) async-start(s8[14680064]{0:T(1024)(128)(4,1)} %bitcast.12), calls=%async_computation.5 | async-start | bytes 4194304
  26.9 1.4 %collective-permute-start = (f32[16,2048]{1,0:T(8,128)S(1)}, f32[16,2048]{1,0:T(8,128)S(1)}, u32[]{:S(2)}, u32[]{:S(2)}) collective-permute-start(f32[16,2048]{1,0:T(8,128)S(1)} %fusion.14), channel_id=1, source_target_pairs={{0,1},{1,0},{2,3},{3,2},{4,5},{5,4},{6,7},{7,6},{8,9},{9,8},{10,11... | collective-permute-start | bytes 393224 | tf_op jit(solution)/shard_map/ppermute | solution.py:35
  26.9 1.5 %collective-permute-start.1 = (f32[16,2048]{1,0:T(8,128)S(1)}, f32[16,2048]{1,0:T(8,128)S(1)}, u32[]{:S(2)}, u32[]{:S(2)}) collective-permute-start(f32[16,2048]{1,0:T(8,128)S(1)} %fusion.15), channel_id=1, source_target_pairs={{0,1},{1,0},{2,3},{3,2},{4,5},{5,4},{6,7},{7,6},{8,9},{9,8},{10,11... | collective-permute-start | bytes 393224 | tf_op jit(solution)/shard_map/ppermute | solution.py:36

commit v2 on v1

v2 whole, which is shorter than its diff:
```python
import functools

import jax
import jax.numpy as jnp
from jax import lax
from jax.experimental import pallas as pl
from jax.experimental.pallas import tpu as pltpu
from jax.sharding import PartitionSpec as P

FLIGHT = 8
CAP = 2
TILE = 512
AHEAD = 450
SMALL = pltpu.CompilerParams(vmem_limit_bytes=4 << 20)
VMEM = pl.BlockSpec(memory_space=pltpu.VMEM)


def near(array):
    return pltpu.with_memory_space_constraint(array, pltpu.VMEM)


def call(kernel, out_shape, *operands, flops=0):
    return pl.pallas_call(
        kernel,
        out_shape=out_shape,
        in_specs=[VMEM] * len(operands),
        out_specs=jax.tree.map(lambda _: VMEM, out_shape),
        compiler_params=SMALL,
        cost_estimate=pl.CostEstimate(flops=flops, bytes_accessed=0, transcendentals=0),
        name=kernel.__name__,
    )(*operands)


def placing(routes, slots):
    rows = routes.shape[1]
    slot = lax.broadcasted_iota(jnp.int32, (slots, rows), 0)
    expert = lax.div(slot, CAP)
    chosen = (routes[0:1, :] == expert).astype(jnp.float32)
    for k in range(1, routes.shape[0]):
        chosen += (routes[k : k + 1, :] == expert).astype(jnp.float32)
    earlier = (
        lax.broadcasted_iota(jnp.int32, (rows, rows), 0)
        < lax.broadcasted_iota(jnp.int32, (rows, rows), 1)
    ).astype(jnp.float32)
    rank = jnp.dot(chosen, earlier, preferred_element_type=jnp.float32)
    return chosen * (rank == (slot - expert * CAP).astype(jnp.float32)).astype(jnp.float32)


def pack(routes_ref, rows_ref, out_ref):
    experts, cap, width = out_ref.shape
    place = placing(routes_ref[...], experts * cap).astype(jnp.bfloat16)
    packed = jnp.dot(place, rows_ref[...], preferred_element_type=jnp.float32).astype(
        out_ref.dtype
    )
    out_ref[...] = packed.reshape(out_ref.shape)


def gate_up(rows_ref, gate_ref, up_ref, gate_out, up_out):
    columns = gate_ref.shape[1]
    tile = min(TILE, columns)
    rows = rows_ref[...].reshape(-1, rows_ref.shape[-1])

    @pl.loop(0, columns // tile)
    def _(i):
        at = pl.ds(pl.multiple_of(i * tile, tile), tile)
        gate_out[:, at] = jnp.dot(rows, gate_ref[:, at], preferred_element_type=jnp.float32)
        up_out[:, at] = jnp.dot(rows, up_ref[:, at], preferred_element_type=jnp.float32)


def down(gate_ref, gate_other, up_ref, up_other, down_ref, out_ref):
    gate = gate_ref[...] + gate_other[...]
    up = up_ref[...] + up_other[...]
    hidden = (gate / (1.0 + jnp.exp(-gate)) * up).astype(jnp.bfloat16)
    columns = down_ref.shape[1]
    tile = min(TILE, columns)

    @pl.loop(0, columns // tile)
    def _(i):
        at = pl.ds(pl.multiple_of(i * tile, tile), tile)
        part = jnp.dot(hidden, down_ref[:, at], preferred_element_type=jnp.float32)
        out_ref[:, :, at] = part.astype(out_ref.dtype).reshape(*out_ref.shape[:2], tile)


def unpack(routes_ref, gates_ref, slots_ref, out_ref):
    experts, cap, width = slots_ref.shape
    routes = routes_ref[...]
    gates = gates_ref[...]
    place = placing(routes, experts * cap)
    slot = lax.broadcasted_iota(jnp.int32, place.shape, 0)
    expert = lax.div(slot, CAP)
    weight = jnp.zeros(place.shape, jnp.float32)
    for k in range(routes.shape[0]):
        weight += jnp.where(routes[k : k + 1, :] == expert, gates[k : k + 1, :], 0.0)
    out_ref[...] = lax.dot_general(
        place * weight,
        slots_ref[...].reshape(experts * cap, width).astype(jnp.float32),
        (((0,), (0,)), ((), ())),
        precision=lax.Precision.HIGHEST,
        preferred_element_type=jnp.float32,
    ).astype(out_ref.dtype)


def per_device(moe_in, routes, gate_weights, w_gate, w_up, w_down):
    rows, width = moe_in.shape
    routes_t, gates_t = routes.T, gate_weights.T
    n = lax.axis_size("expert")
    copies = n // FLIGHT
    outgoing = call(
        pack, jax.ShapeDtypeStruct((FLIGHT, CAP, width), moe_in.dtype), routes_t, moe_in,
        flops=AHEAD * (w_gate.nbytes + w_up.nbytes + w_down.nbytes),
    )
    if copies > 1:
        outgoing = jnp.broadcast_to(outgoing[:, None], (FLIGHT, copies, CAP, width)).reshape(
            n, CAP, width
        )
    arrived = lax.all_to_all(outgoing, "expert", split_axis=0, concat_axis=0, tiled=True)
    pre = jax.ShapeDtypeStruct((n * CAP, w_gate.shape[1]), jnp.float32)
    gate_part, up_part = call(
        gate_up, (pre, pre), arrived, near(w_gate), near(w_up), flops=4 * n * CAP * w_gate.size
    )
    cores = lax.axis_size("head")
    swap = [(i, (i + 1) % cores) for i in range(cores)]
    gate_other, up_other = (lax.ppermute(x, "head", swap) for x in (gate_part, up_part))
    partial_out = call(
        down,
        jax.ShapeDtypeStruct((n, CAP, width), moe_in.dtype),
        gate_part, gate_other, up_part, up_other, near(w_down),
        flops=2 * n * CAP * w_down.size,
    )
    returned = lax.all_to_all(partial_out, "expert", split_axis=0, concat_axis=0, tiled=True)
    if copies > 1:
        returned = jnp.sum(
            returned.reshape(FLIGHT, copies, CAP, width).astype(jnp.float32), axis=1
        )
    return call(unpack, jax.ShapeDtypeStruct((rows, width), moe_in.dtype), routes_t, gates_t, returned)


def solution(mesh):
    in_specs = (
        P(("groups", "expert"), "head"),
        P(("groups", "expert"), None),
        P(("groups", "expert"), None),
        P("head", "expert"),
        P("head", "expert"),
        P("expert", "head"),
    )
    out_specs = P(("groups", "expert"), "head")
    return jax.shard_map(
        per_device, mesh=mesh, in_specs=in_specs, out_specs=out_specs, check_vma=False
    )
```

time: 42.1 us -> 36.2 us (0.86)
  matrix products: 12.4 us -> 0 us
  Pallas kernels: 0 us -> 8.46 us
  local copies, waits for them, and re-layouts: 3.11 us -> 1.53 us
  other arithmetic: 0.81 us -> 0.01 us
  blocking collectives: 23.9 us -> 24.4 us
    dot_general x5 -> x0, matrix products: 12.4 us -> none  [the longest x1 7.33 us: per_device(): up_part = jnp.dot(arrived_rows, w_up, preferred_element_type=jnp.float32)]
    pallas_call x0 -> x4, Pallas kernels: none -> 8.46 us  [call(): pl.pallas_call(kernel, out_shape=out_shape, in_specs=[VMEM] * len(operand...]
    unnamed x12 -> x20, local copies, waits for them, and re-layouts: 2.91 us -> 1.53 us
    reduce_sum x1 -> x0, other arithmetic: 0.78 us -> none  [per_device(): gate_hit = jnp.sum(matched * gate_weights[:, :, None], axis=1)]
where the time goes in v2:
time: 36.2 us; the launch traced here: 36 us
  blocking collectives  24.4 us (67%)
  Pallas kernels  8.46 us (23%)
  local copies, waits for them, and re-layouts  1.53 us (4%)
  waiting for transfers between devices  1.02 us (3%)
  starting transfers between devices  0.51 us (1%)
    all_to_all x1, blocking collectives, per_device(): lax.all_to_all(outgoing, 'expert', split_axis=0, concat_axis=0, tiled=True)  14.5 us
    all_to_all x1, blocking collectives, per_device(): lax.all_to_all(partial_out, 'expert', split_axis=0, concat_axis=0, tiled=...  9.9 us
    pallas_call x4, Pallas kernels, call(): pl.pallas_call(kernel, out_shape=out_shape, in_specs=[VMEM] * len(operand...  8.46 us
    unnamed x20, local copies, waits for them, and re-layouts  1.53 us
    ppermute x2, waiting for transfers between devices, per_device(): lax.ppermute(x, 'head', swap)  1.02 us
  transfers between devices with their start and end apart: 2, of which 2 were waited for; matrix products, arithmetic and copies ran while one was open for 0% of the time, Pallas kernels for 0%

profile of v2, /device:TPU:0, one launch (start us, length us, event | category | flops | bytes accessed | tf_op | source)
XLA Modules:
  0.0 36.0 jit_solution(3120906369230872844)
XLA Ops:
  0.0 0.0 copy-start.2
  0.0 0.7 %copy-done.2 = s32[8,2]{0,1:T(2,128)S(1)} copy-done((s32[8,2]{0,1:T(2,128)S(1)}, s32[8,2]{0,1:T(2,128)}, u32[]{:S(2)}) %copy-start.2) | copy-done | bytes 88
  0.7 0.0 copy-start.5
  0.7 0.8 %copy-done.5 = bf16[8,3584]{1,0:T(8,128)(2,1)S(1)} copy-done((bf16[8,3584]{1,0:T(8,128)(2,1)S(1)}, bf16[8,3584]{1,0:T(8,128)(2,1)}, u32[]{:S(2)}) %copy-start.5) | copy-done | bytes 57368
  1.5 0.0 copy-start
  1.5 0.0 slice-start.2
  1.5 0.3 pack.1
  1.8 14.5 %all_to_all.10.rows_ref = bf16[8,2,3584]{2,1,0:T(2,128)(2,1)S(1)} all-to-all(bf16[8,2,3584]{2,1,0:T(2,128)(2,1)S(1)} %pack.1), channel_id=1, replica_groups=mesh['groups'=2,'expert'=8,'head'=2] {'expert'}, dimensions={0} | all-to-all | bytes 229376 | tf_op jit(solution)/shard_map/all_to_all | solution.py:116
  16.4 0.0 copy-done
  16.4 0.0 copy-done.1
  16.4 4.3 %gate_up.1 = (f32[16,2048]{1,0:T(8,128)S(1)}, f32[16,2048]{1,0:T(8,128)S(1)}) custom-call(bf16[8,2,3584]{2,1,0:T(2,128)(2,1)S(1)} %all_to_all.10.rows_ref, bf16[3584,2048]{1,0:T(8,128)(2,1)S(1)} %copy-done, bf16[3584,2048]{1,0:T(8,128)(2,1)S(1)} %copy-done.1), custom_call_target="tpu_custom_call" | custom-call | flops 469762048 | tf_op jit(solution)/shard_map/gate_up/pallas_call | solution.py:23
  20.6 0.0 collective-permute-start
  20.6 0.5 %collective-permute-start.1 = (f32[16,2048]{1,0:T(8,128)S(1)}, f32[16,2048]{1,0:T(8,128)S(1)}, u32[]{:S(2)}, u32[]{:S(2)}) collective-permute-start(f32[16,2048]{1,0:T(8,128)S(1)} %get-tuple-element.8.up_ref), channel_id=1, source_target_pairs={{0,1},{1,0},{2,3},{3,2},{4,5},{5,4},{6,7},{7,6},{8,9},{9,8},{10,11... | collective-permute-start | bytes 393224 | tf_op jit(solution)/shard_map/ppermute | solution.py:123
  21.2 0.8 %collective-permute-done.gate_other = f32[16,2048]{1,0:T(8,128)S(1)} collective-permute-done((f32[16,2048]{1,0:T(8,128)S(1)}, f32[16,2048]{1,0:T(8,128)S(1)}, u32[]{:S(2)}, u32[]{:S(2)}) %collective-permute-start) | collective-permute-done | bytes 131104 | tf_op jit(solution)/shard_map/ppermute | solution.py:123
  22.0 0.2 collective-permute-done.1.up_other
  22.2 0.0 slice-done
  22.2 0.0 slice-done.1
  22.2 0.0 slice-done.2
  22.2 0.0 slice-done.3
  22.2 2.8 %down.1 = bf16[8,2,3584]{2,1,0:T(2,128)(2,1)S(1)} custom-call(f32[16,2048]{1,0:T(8,128)S(1)} %get-tuple-element.7.gate_ref, f32[16,2048]{1,0:T(8,128)S(1)} %collective-permute-done.gate_other, f32[16,2048]{1,0:T(8,128)S(1)} %get-tuple-element.8.up_ref, f32[16,2048]{1,0:T(8,128)S(1)} %collective-permute-done.1.up_other, bf16[2048,3584]{1,0:T(8,128)(2,1)S(1)} %bitcast.3), custom_call_target="tpu_custom_call" | custom-call | flops 234881024 | tf_op jit(solution)/shard_map/down/pallas_call | solution.py:23
  25.0 9.9 %all_to_all.11.slots_ref = bf16[8,2,3584]{2,1,0:T(2,128)(2,1)S(1)} all-to-all(bf16[8,2,3584]{2,1,0:T(2,128)(2,1)S(1)} %down.1), channel_id=1, replica_groups=mesh['groups'=2,'expert'=8,'head'=2] {'expert'}, dimensions={0} | all-to-all | bytes 229376 | tf_op jit(solution)/shard_map/all_to_all | solution.py:130
  34.9 0.0 copy-done.3
  34.9 0.0 copy-done.4
  34.9 1.1 %unpack.1 = bf16[8,3584]{1,0:T(8,128)(2,1)} custom-call(s32[2,8]{1,0:T(2,128)S(1)} %bitcast.5, f32[2,8]{1,0:T(2,128)S(1)} %bitcast.6, bf16[8,2,3584]{2,1,0:T(2,128)(2,1)S(1)} %all_to_all.11.slots_ref), custom_call_target="tpu_custom_call" | custom-call | tf_op jit(solution)/shard_map/unpack/pallas_call | solution.py:23
  (7 shorter events, 0.0 us)
Async XLA Ops:
  0.0 0.7 %copy-start.2 = (s32[8,2]{0,1:T(2,128)S(1)}, s32[8,2]{0,1:T(2,128)}, u32[]{:S(2)}) copy-start(s32[8,2]{0,1:T(2,128)} %param.7) | copy-start | bytes 196
  0.7 0.8 %copy-start.5 = (bf16[8,3584]{1,0:T(8,128)(2,1)S(1)}, bf16[8,3584]{1,0:T(8,128)(2,1)}, u32[]{:S(2)}) copy-start(bf16[8,3584]{1,0:T(8,128)(2,1)} %rows_ref.1) | copy-start | bytes 172036
  1.5 14.9 %copy-start = (bf16[3584,2048]{1,0:T(8,128)(2,1)S(1)}, bf16[3584,2048]{1,0:T(8,128)(2,1)}, u32[]{:S(2)}) copy-start(bf16[3584,2048]{1,0:T(8,128)(2,1)} %gate_ref.1) | copy-start | bytes 44040196
  1.5 14.9 %copy-start.1 = (bf16[3584,2048]{1,0:T(8,128)(2,1)S(1)}, bf16[3584,2048]{1,0:T(8,128)(2,1)}, u32[]{:S(2)}) copy-start(bf16[3584,2048]{1,0:T(8,128)(2,1)} %up_ref.1) | copy-start | bytes 44040196
  1.5 20.7 %slice-start = ((s8[14680064]{0:T(1024)(128)(4,1)}), s8[4194304]{0:T(1024)(128)(4,1)S(1)}, s32[]{:S(2)}) async-start(s8[14680064]{0:T(1024)(128)(4,1)} %bitcast.2), calls=%async_computation.2 | async-start | bytes 8388608
  1.5 20.7 %slice-start.1 = ((s8[14680064]{0:T(1024)(128)(4,1)}), s8[4194304]{0:T(1024)(128)(4,1)S(1)}, s32[]{:S(2)}) async-start(s8[14680064]{0:T(1024)(128)(4,1)} %bitcast.2), calls=%async_computation.3 | async-start | bytes 8388608
  1.5 20.7 %slice-start.2 = ((s8[14680064]{0:T(1024)(128)(4,1)}), s8[4194304]{0:T(1024)(128)(4,1)S(1)}, s32[]{:S(2)}) async-start(s8[14680064]{0:T(1024)(128)(4,1)} %bitcast.2), calls=%async_computation.4 | async-start | bytes 8388608
  16.4 5.8 %slice-start.3 = ((s8[14680064]{0:T(1024)(128)(4,1)}), s8[2097152]{0:T(1024)(128)(4,1)S(1)}, s32[]{:S(2)}) async-start(s8[14680064]{0:T(1024)(128)(4,1)} %bitcast.2), calls=%async_computation.5 | async-start | bytes 4194304
  20.6 14.3 %copy-start.3 = (s32[8,2]{0,1:T(2,128)S(1)}, s32[8,2]{0,1:T(2,128)}, u32[]{:S(2)}) copy-start(s32[8,2]{0,1:T(2,128)} %param.7) | copy-start | bytes 196
  20.6 14.3 %copy-start.4 = (f32[8,2]{0,1:T(2,128)S(1)}, f32[8,2]{0,1:T(2,128)}, u32[]{:S(2)}) copy-start(f32[8,2]{0,1:T(2,128)} %param.8) | copy-start | bytes 196
  20.6 1.4 %collective-permute-start = (f32[16,2048]{1,0:T(8,128)S(1)}, f32[16,2048]{1,0:T(8,128)S(1)}, u32[]{:S(2)}, u32[]{:S(2)}) collective-permute-start(f32[16,2048]{1,0:T(8,128)S(1)} %get-tuple-element.7.gate_ref), channel_id=1, source_target_pairs={{0,1},{1,0},{2,3},{3,2},{4,5},{5,4},{6,7},{7,6},{8,9},{9,8},{10,11... | collective-permute-start | bytes 393224 | tf_op jit(solution)/shard_map/ppermute | solution.py:123
  20.6 1.5 %collective-permute-start.1 = (f32[16,2048]{1,0:T(8,128)S(1)}, f32[16,2048]{1,0:T(8,128)S(1)}, u32[]{:S(2)}, u32[]{:S(2)}) collective-permute-start(f32[16,2048]{1,0:T(8,128)S(1)} %get-tuple-element.8.up_ref), channel_id=1, source_target_pairs={{0,1},{1,0},{2,3},{3,2},{4,5},{5,4},{6,7},{7,6},{8,9},{9,8},{10,11... | collective-permute-start | bytes 393224 | tf_op jit(solution)/shard_map/ppermute | solution.py:123

commit v3 on v2

v3 whole, which is shorter than its diff:
```python
import functools

import jax
import jax.numpy as jnp
from jax import lax
from jax.experimental import pallas as pl
from jax.experimental.pallas import tpu as pltpu
from jax.sharding import PartitionSpec as P

FLIGHT = 8
CAP = 2
TILE = 512
LANES = 128
AHEAD = 300
SMALL = pltpu.CompilerParams(vmem_limit_bytes=4 << 20)
VMEM = pl.BlockSpec(memory_space=pltpu.VMEM)


def near(array):
    return pltpu.with_memory_space_constraint(array, pltpu.VMEM)


def far(array):
    return pltpu.with_memory_space_constraint(array, pltpu.HBM)


def call(kernel, out_shape, *operands, flops=0):
    return pl.pallas_call(
        kernel,
        out_shape=out_shape,
        in_specs=[VMEM] * len(operands),
        out_specs=jax.tree.map(lambda _: VMEM, out_shape),
        compiler_params=SMALL,
        cost_estimate=pl.CostEstimate(flops=flops, bytes_accessed=0, transcendentals=0),
        name=getattr(kernel, "func", kernel).__name__,
    )(*operands)


def placing(routes, slots):
    rows = routes.shape[1]
    slot = lax.broadcasted_iota(jnp.int32, (slots, rows), 0)
    expert = lax.div(slot, CAP)
    chosen = (routes[0:1, :] == expert).astype(jnp.float32)
    for k in range(1, routes.shape[0]):
        chosen += (routes[k : k + 1, :] == expert).astype(jnp.float32)
    earlier = (
        lax.broadcasted_iota(jnp.int32, (rows, rows), 0)
        < lax.broadcasted_iota(jnp.int32, (rows, rows), 1)
    ).astype(jnp.float32)
    rank = jnp.dot(chosen, earlier, preferred_element_type=jnp.float32)
    return chosen * (rank == (slot - expert * CAP).astype(jnp.float32)).astype(jnp.float32)


def pack(routes_hbm, rows_hbm, out_ref, routes_ref, rows_ref, sems):
    loads = [
        pltpu.make_async_copy(routes_hbm, routes_ref, sems.at[0]),
        pltpu.make_async_copy(rows_hbm, rows_ref, sems.at[1]),
    ]
    for load in loads:
        load.start()
    loads[0].wait()
    experts, cap, width = out_ref.shape
    place = placing(routes_ref[...], experts * cap).astype(jnp.bfloat16)
    loads[1].wait()
    packed = jnp.dot(place, rows_ref[...], preferred_element_type=jnp.float32).astype(
        out_ref.dtype
    )
    out_ref[...] = packed.reshape(out_ref.shape)


def gate_up(part, rows_ref, gate_ref, up_ref, out_ref):
    columns = out_ref.shape[2]
    tile = min(TILE, columns)
    rows = rows_ref[...].reshape(-1, rows_ref.shape[-1])
    for start in range(0, columns, tile):
        for k, weights in enumerate((gate_ref, up_ref)):
            out_ref[k, :, start : start + tile] = jnp.dot(
                rows,
                weights[:, part * columns + start : part * columns + start + tile],
                preferred_element_type=jnp.float32,
            )


def spread(routes, gates, slots):
    place = placing(routes, slots)
    expert = lax.div(lax.broadcasted_iota(jnp.int32, place.shape, 0), CAP)
    weight = jnp.zeros(place.shape, jnp.float32)
    for k in range(routes.shape[0]):
        weight += jnp.where(routes[k : k + 1, :] == expert, gates[k : k + 1, :], 0.0)
    rest, terms = place * weight, []
    for _ in range(3):
        terms.append(rest.astype(jnp.bfloat16))
        rest = rest - terms[-1].astype(jnp.float32)
    return jnp.concatenate(terms, axis=1)


def down(part, last, down_ref, own_ref, other_ref, *refs):
    columns = own_ref.shape[2]
    gate = own_ref[0] + other_ref[0]
    up = own_ref[1] + other_ref[1]
    hidden = (gate / (1.0 + jnp.exp(-gate)) * up).astype(jnp.bfloat16)
    width = down_ref.shape[1]
    tile = min(TILE, width)
    if last:
        *totals, routes_ref, gates_ref, out_ref, terms_ref = refs
        terms_ref[...] = spread(routes_ref[...], gates_ref[...], terms_ref.shape[0])
    else:
        *totals, out_ref = refs
    for start in range(0, width, tile):
        at = slice(start, start + tile)
        total = jnp.dot(
            hidden,
            down_ref[part * columns : (part + 1) * columns, at],
            preferred_element_type=jnp.float32,
        )
        if totals:
            total += totals[0][:, at]
        out_ref[..., at] = total.astype(out_ref.dtype).reshape(*out_ref.shape[:-1], tile)


def unpack(terms_ref, slots_ref, out_ref):
    experts, cap, width = slots_ref.shape
    sums = lax.dot_general(
        terms_ref[...],
        slots_ref[...].astype(jnp.bfloat16).reshape(experts * cap, width),
        (((0,), (0,)), ((), ())),
        preferred_element_type=jnp.float32,
    )
    rows = out_ref.shape[0]
    out_ref[...] = (sums[:rows] + sums[rows : 2 * rows] + sums[2 * rows :]).astype(out_ref.dtype)


def per_device(moe_in, routes, gate_weights, w_gate, w_up, w_down):
    rows, width = moe_in.shape
    routes_t, gates_t = routes.T, gate_weights.T
    n = lax.axis_size("expert")
    copies = n // FLIGHT
    outgoing = pl.pallas_call(
        pack,
        out_shape=jax.ShapeDtypeStruct((FLIGHT, CAP, width), moe_in.dtype),
        in_specs=[pl.BlockSpec(memory_space=pltpu.HBM)] * 2,
        out_specs=VMEM,
        scratch_shapes=[
            pltpu.VMEM(routes_t.shape, routes_t.dtype),
            pltpu.VMEM(moe_in.shape, moe_in.dtype),
            pltpu.SemaphoreType.DMA((2,)),
        ],
        compiler_params=SMALL,
        cost_estimate=pl.CostEstimate(
            flops=AHEAD * (w_gate.nbytes + w_up.nbytes + w_down.nbytes),
            bytes_accessed=0,
            transcendentals=0,
        ),
        name="pack",
    )(far(routes_t), far(moe_in))
    if copies > 1:
        outgoing = jnp.broadcast_to(outgoing[:, None], (FLIGHT, copies, CAP, width)).reshape(
            n, CAP, width
        )
    arrived = lax.all_to_all(outgoing, "expert", split_axis=0, concat_axis=0, tiled=True)
    columns = w_gate.shape[1]
    parts = 2 if columns % (2 * LANES) == 0 else 1
    cores = lax.axis_size("head")
    swap = [(i, (i + 1) % cores) for i in range(cores)]
    near_gate, near_up, near_down = near(w_gate), near(w_up), near(w_down)
    own, other = [], []
    for part in range(parts):
        own.append(
            call(
                functools.partial(gate_up, part),
                jax.ShapeDtypeStruct((2, n * CAP, columns // parts), jnp.float32),
                arrived, near_gate, near_up,
                flops=4 * n * CAP * w_gate.size // parts,
            )
        )
        other.append(lax.ppermute(own[-1], "head", swap))
    totals = ()
    for part in range(parts - 1):
        totals = (
            call(
                functools.partial(down, part, False),
                jax.ShapeDtypeStruct((n * CAP, width), jnp.float32),
                near_down, own[part], other[part], *totals,
                flops=2 * n * CAP * w_down.size // parts,
            ),
        )
    partial_out, terms = call(
        functools.partial(down, parts - 1, True),
        (
            jax.ShapeDtypeStruct((n, CAP, width), moe_in.dtype),
            jax.ShapeDtypeStruct((FLIGHT * CAP, 3 * rows), jnp.bfloat16),
        ),
        near_down, own[-1], other[-1], *totals, routes_t, gates_t,
        flops=2 * n * CAP * w_down.size // parts,
    )
    returned = lax.all_to_all(partial_out, "expert", split_axis=0, concat_axis=0, tiled=True)
    if copies > 1:
        returned = jnp.sum(
            returned.reshape(FLIGHT, copies, CAP, width).astype(jnp.float32), axis=1
        )
    return call(unpack, jax.ShapeDtypeStruct((rows, width), moe_in.dtype), terms, returned)


def solution(mesh):
    in_specs = (
        P(("groups", "expert"), "head"),
        P(("groups", "expert"), None),
        P(("groups", "expert"), None),
        P("head", "expert"),
        P("head", "expert"),
        P("expert", "head"),
    )
    out_specs = P(("groups", "expert"), "head")
    return jax.shard_map(
        per_device, mesh=mesh, in_specs=in_specs, out_specs=out_specs, check_vma=False
    )
```

time: 36.2 us -> 34 us (0.939)
  waiting for transfers between devices: 1.02 us -> 0.01 us
  local copies, waits for them, and re-layouts: 1.53 us -> 0.94 us
    pallas_call x4 -> x5, Pallas kernels: 8.46 us -> 7.01 us  [call(): pl.pallas_call(kernel, out_shape=out_shape, in_specs=[VMEM] * len(operand...]
    pallas_call x0 -> x1, Pallas kernels: none -> 1.16 us  [per_device(): pl.pallas_call(pack, out_shape=jax.ShapeDtypeStruct((FLIGHT, CAP, width),...]
    ppermute x2, waiting for transfers between devices: 1.02 us -> 0.01 us  [per_device(): other.append(lax.ppermute(own[-1], 'head', swap))]
    unnamed x20 -> x16, local copies, waits for them, and re-layouts: 1.53 us -> 0.94 us
  transfers between devices with their start and end apart: 2 -> 2, of which waited for: 2 -> 0; matrix products, arithmetic and copies ran while one was open for 0% -> 0% of each run, Pallas kernels for 0% -> 9%
where the time goes in v3:
time: 34 us; the launch traced here: 33.8 us
  blocking collectives  24.2 us (71%)
  Pallas kernels  8.17 us (24%)
  local copies, waits for them, and re-layouts  0.94 us (3%)
  starting transfers between devices  0.52 us (2%)
    all_to_all x1, blocking collectives, per_device(): lax.all_to_all(outgoing, 'expert', split_axis=0, concat_axis=0, tiled=True)  14.5 us
    all_to_all x1, blocking collectives, per_device(): lax.all_to_all(partial_out, 'expert', split_axis=0, concat_axis=0, tiled=...  9.61 us
    pallas_call x5, Pallas kernels, call(): pl.pallas_call(kernel, out_shape=out_shape, in_specs=[VMEM] * len(operand...  7.01 us
    pallas_call x1, Pallas kernels, per_device(): pl.pallas_call(pack, out_shape=jax.ShapeDtypeStruct((FLIGHT, CAP, width),...  1.16 us
    unnamed x16, local copies, waits for them, and re-layouts  0.94 us
  transfers between devices with their start and end apart: 2, of which 0 were waited for; matrix products, arithmetic and copies ran while one was open for 0% of the time, Pallas kernels for 9%

profile of v3, /device:TPU:0, one launch (start us, length us, event | category | flops | bytes accessed | tf_op | source)
XLA Modules:
  0.0 33.8 jit_solution(5178061967399059002)
XLA Ops:
  0.0 0.0 copy-start
  0.0 0.0 copy-start.1
  0.0 1.2 %pack.1 = bf16[8,2,3584]{2,1,0:T(2,128)(2,1)S(1)} custom-call(s32[2,8]{1,0:T(2,128)} %bitcast.4, bf16[8,3584]{1,0:T(8,128)(2,1)} %rows_hbm.1), custom_call_target="tpu_custom_call" | custom-call | flops 13212057600 | tf_op jit(solution)/shard_map/pack/pallas_call | solution.py:138
  1.2 14.5 %all_to_all.10.rows_ref = bf16[8,2,3584]{2,1,0:T(2,128)(2,1)S(1)} all-to-all(bf16[8,2,3584]{2,1,0:T(2,128)(2,1)S(1)} %pack.1), channel_id=1, replica_groups=mesh['groups'=2,'expert'=8,'head'=2] {'expert'}, dimensions={0} | all-to-all | bytes 229376 | tf_op jit(solution)/shard_map/all_to_all | solution.py:160
  15.7 0.0 copy-done
  15.7 0.0 copy-done.1
  15.7 0.0 slice-start
  15.7 0.0 slice-start.1
  15.7 2.0 %gate_up.3.own_ref = f32[2,16,1024]{2,1,0:T(8,128)S(1)} custom-call(bf16[8,2,3584]{2,1,0:T(2,128)(2,1)S(1)} %all_to_all.10.rows_ref, bf16[3584,2048]{1,0:T(8,128)(2,1)S(1)} %copy-done, bf16[3584,2048]{1,0:T(8,128)(2,1)S(1)} %copy-done.1), custom_call_target="tpu_custom_call" | custom-call | flops 234881024 | tf_op jit(solution)/shard_map/gate_up/pallas_call | solution.py:28
  17.7 0.0 collective-permute-start.1
  17.8 2.0 %gate_up.2.own_ref = f32[2,16,1024]{2,1,0:T(8,128)S(1)} custom-call(bf16[8,2,3584]{2,1,0:T(2,128)(2,1)S(1)} %all_to_all.10.rows_ref, bf16[3584,2048]{1,0:T(8,128)(2,1)S(1)} %copy-done, bf16[3584,2048]{1,0:T(8,128)(2,1)S(1)} %copy-done.1), custom_call_target="tpu_custom_call" | custom-call | flops 234881024 | tf_op jit(solution)/shard_map/gate_up/pallas_call | solution.py:28
  19.8 0.5 %collective-permute-start = (f32[2,16,1024]{2,1,0:T(8,128)S(1)}, f32[2,16,1024]{2,1,0:T(8,128)S(1)}, u32[]{:S(2)}, u32[]{:S(2)}) collective-permute-start(f32[2,16,1024]{2,1,0:T(8,128)S(1)} %gate_up.2.own_ref), channel_id=1, source_target_pairs={{0,1},{1,0},{2,3},{3,2},{4,5},{5,4},{6,7},{7,6},{8,9},{9,8},{10,11... | collective-permute-start | bytes 393224 | tf_op jit(solution)/shard_map/ppermute | solution.py:176
  20.3 0.0 collective-permute-done.1.other_ref
  20.3 0.0 slice-done
  20.3 0.0 slice-done.1
  20.3 0.3 slice-done.2
  20.6 0.6 %slice-done.3 = s8[2097152]{0:T(1024)(128)(4,1)S(1)} async-done(((s8[14680064]{0:T(1024)(128)(4,1)}), s8[2097152]{0:T(1024)(128)(4,1)S(1)}, s32[]{:S(2)}) %slice-start.3) | async-done | bytes 2097176
  21.2 1.1 %down.2.refs_0_ = f32[16,3584]{1,0:T(8,128)S(1)} custom-call(bf16[2048,3584]{1,0:T(8,128)(2,1)S(1)} %bitcast.3, f32[2,16,1024]{2,1,0:T(8,128)S(1)} %gate_up.3.own_ref, f32[2,16,1024]{2,1,0:T(8,128)S(1)} %collective-permute-done.1.other_ref), custom_call_target="tpu_custom_call" | custom-call | flops 117440512 | tf_op jit(solution)/shard_map/down/pallas_call | solution.py:28
  22.2 0.0 collective-permute-done.other_ref
  22.3 0.0 copy-done.2
  22.3 0.0 copy-done.3
  22.3 1.1 %down.3 = (bf16[8,2,3584]{2,1,0:T(2,128)(2,1)S(1)}, bf16[16,24]{1,0:T(8,128)(2,1)S(1)}) custom-call(bf16[2048,3584]{1,0:T(8,128)(2,1)S(1)} %bitcast.3, f32[2,16,1024]{2,1,0:T(8,128)S(1)} %gate_up.2.own_ref, f32[2,16,1024]{2,1,0:T(8,128)S(1)} %collective-permute-done.other_ref, f32[16,3584]{1,0:T(8,128)S(1)} %down.2.refs_0_, s32[2,8]{1,0:T(2,128)S(1)} %bitcast.5, ...), custom_call_target="tpu_custom_call" | custom-call | flops 117440512 | tf_op jit(solution)/shard_map/down/pallas_call | solution.py:28
  23.4 9.6 %all_to_all.11.slots_ref = bf16[8,2,3584]{2,1,0:T(2,128)(2,1)S(1)} all-to-all(bf16[8,2,3584]{2,1,0:T(2,128)(2,1)S(1)} %get-tuple-element.8), channel_id=1, replica_groups=mesh['groups'=2,'expert'=8,'head'=2] {'expert'}, dimensions={0} | all-to-all | bytes 229376 | tf_op jit(solution)/shard_map/all_to_all | solution.py:196
  33.0 0.9 %unpack.1 = bf16[8,3584]{1,0:T(8,128)(2,1)} custom-call(bf16[16,24]{1,0:T(8,128)(2,1)S(1)} %get-tuple-element.7.terms_ref, bf16[8,2,3584]{2,1,0:T(2,128)(2,1)S(1)} %all_to_all.11.slots_ref), custom_call_target="tpu_custom_call" | custom-call | tf_op jit(solution)/shard_map/unpack/pallas_call | solution.py:28
  (5 shorter events, 0.0 us)
Async XLA Ops:
  0.0 15.7 %copy-start = (bf16[3584,2048]{1,0:T(8,128)(2,1)S(1)}, bf16[3584,2048]{1,0:T(8,128)(2,1)}, u32[]{:S(2)}) copy-start(bf16[3584,2048]{1,0:T(8,128)(2,1)} %gate_ref.3) | copy-start | bytes 44040196
  0.0 15.7 %copy-start.1 = (bf16[3584,2048]{1,0:T(8,128)(2,1)S(1)}, bf16[3584,2048]{1,0:T(8,128)(2,1)}, u32[]{:S(2)}) copy-start(bf16[3584,2048]{1,0:T(8,128)(2,1)} %up_ref.3) | copy-start | bytes 44040196
  15.7 4.6 %slice-start = ((s8[14680064]{0:T(1024)(128)(4,1)}), s8[4194304]{0:T(1024)(128)(4,1)S(1)}, s32[]{:S(2)}) async-start(s8[14680064]{0:T(1024)(128)(4,1)} %bitcast.2), calls=%async_computation.2 | async-start | bytes 8388608
  15.7 4.6 %slice-start.1 = ((s8[14680064]{0:T(1024)(128)(4,1)}), s8[4194304]{0:T(1024)(128)(4,1)S(1)}, s32[]{:S(2)}) async-start(s8[14680064]{0:T(1024)(128)(4,1)} %bitcast.2), calls=%async_computation.3 | async-start | bytes 8388608
  17.7 2.9 %slice-start.2 = ((s8[14680064]{0:T(1024)(128)(4,1)}), s8[4194304]{0:T(1024)(128)(4,1)S(1)}, s32[]{:S(2)}) async-start(s8[14680064]{0:T(1024)(128)(4,1)} %bitcast.2), calls=%async_computation.4 | async-start | bytes 8388608
  17.7 3.5 %slice-start.3 = ((s8[14680064]{0:T(1024)(128)(4,1)}), s8[2097152]{0:T(1024)(128)(4,1)S(1)}, s32[]{:S(2)}) async-start(s8[14680064]{0:T(1024)(128)(4,1)} %bitcast.2), calls=%async_computation.5 | async-start | bytes 4194304
  17.7 2.5 %collective-permute-start.1 = (f32[2,16,1024]{2,1,0:T(8,128)S(1)}, f32[2,16,1024]{2,1,0:T(8,128)S(1)}, u32[]{:S(2)}, u32[]{:S(2)}) collective-permute-start(f32[2,16,1024]{2,1,0:T(8,128)S(1)} %gate_up.3.own_ref), channel_id=1, source_target_pairs={{0,1},{1,0},{2,3},{3,2},{4,5},{5,4},{6,7},{7,6},{8,9},{9,8},{10,11... | collective-permute-start | bytes 393224 | tf_op jit(solution)/shard_map/ppermute | solution.py:176
  19.8 2.5 %copy-start.2 = (s32[8,2]{0,1:T(2,128)S(1)}, s32[8,2]{0,1:T(2,128)}, u32[]{:S(2)}) copy-start(s32[8,2]{0,1:T(2,128)} %param.7) | copy-start | bytes 196
  19.8 2.5 %copy-start.3 = (f32[8,2]{0,1:T(2,128)S(1)}, f32[8,2]{0,1:T(2,128)}, u32[]{:S(2)}) copy-start(f32[8,2]{0,1:T(2,128)} %param.8) | copy-start | bytes 196
  19.8 2.5 %collective-permute-start = (f32[2,16,1024]{2,1,0:T(8,128)S(1)}, f32[2,16,1024]{2,1,0:T(8,128)S(1)}, u32[]{:S(2)}, u32[]{:S(2)}) collective-permute-start(f32[2,16,1024]{2,1,0:T(8,128)S(1)} %gate_up.2.own_ref), channel_id=1, source_target_pairs={{0,1},{1,0},{2,3},{3,2},{4,5},{5,4},{6,7},{7,6},{8,9},{9,8},{10,11... | collective-permute-start | bytes 393224 | tf_op jit(solution)/shard_map/ppermute | solution.py:176

commit v4 on v3

--- a/solution.py
+++ b/solution.py
@@ -11,6 +11,7 @@
 CAP = 2
 TILE = 512
 LANES = 128
+ORDERS = {8: (4, 2, 7, 6, 0, 1, 3, 5)}
 AHEAD = 300
 SMALL = pltpu.CompilerParams(vmem_limit_bytes=4 << 20)
 VMEM = pl.BlockSpec(memory_space=pltpu.VMEM)
@@ -36,10 +37,18 @@
     )(*operands)
 
 
-def placing(routes, slots):
+def experts_of(order, shape):
+    slot = lax.broadcasted_iota(jnp.int32, shape, 0)
+    block = lax.div(slot, CAP)
+    expert = jnp.zeros(shape, jnp.int32)
+    for place, name in enumerate(order):
+        expert = jnp.where(block == place, name, expert)
+    return expert, slot - block * CAP
+
+
+def placing(routes, order):
     rows = routes.shape[1]
-    slot = lax.broadcasted_iota(jnp.int32, (slots, rows), 0)
-    expert = lax.div(slot, CAP)
+    expert, number = experts_of(order, (len(order) * CAP, rows))
     chosen = (routes[0:1, :] == expert).astype(jnp.float32)
     for k in range(1, routes.shape[0]):
         chosen += (routes[k : k + 1, :] == expert).astype(jnp.float32)
@@ -48,10 +57,10 @@
         < lax.broadcasted_iota(jnp.int32, (rows, rows), 1)
     ).astype(jnp.float32)
     rank = jnp.dot(chosen, earlier, preferred_element_type=jnp.float32)
-    return chosen * (rank == (slot - expert * CAP).astype(jnp.float32)).astype(jnp.float32)
-
-
-def pack(routes_hbm, rows_hbm, out_ref, routes_ref, rows_ref, sems):
+    return chosen * (rank == number.astype(jnp.float32)).astype(jnp.float32)
+
+
+def pack(order, routes_hbm, rows_hbm, out_ref, routes_ref, rows_ref, sems):
     loads = [
         pltpu.make_async_copy(routes_hbm, routes_ref, sems.at[0]),
         pltpu.make_async_copy(rows_hbm, rows_ref, sems.at[1]),
@@ -59,8 +68,7 @@
     for load in loads:
         load.start()
     loads[0].wait()
-    experts, cap, width = out_ref.shape
-    place = placing(routes_ref[...], experts * cap).astype(jnp.bfloat16)
+    place = placing(routes_ref[...], order).astype(jnp.bfloat16)
     loads[1].wait()
     packed = jnp.dot(place, rows_ref[...], preferred_element_type=jnp.float32).astype(
         out_ref.dtype
@@ -81,9 +89,9 @@
             )
 
 
-def spread(routes, gates, slots):
-    place = placing(routes, slots)
-    expert = lax.div(lax.broadcasted_iota(jnp.int32, place.shape, 0), CAP)
+def spread(routes, gates, order):
+    place = placing(routes, order)
+    expert, _ = experts_of(order, place.shape)
     weight = jnp.zeros(place.shape, jnp.float32)
     for k in range(routes.shape[0]):
         weight += jnp.where(routes[k : k + 1, :] == expert, gates[k : k + 1, :], 0.0)
@@ -94,16 +102,16 @@
     return jnp.concatenate(terms, axis=1)
 
 
-def down(part, last, down_ref, own_ref, other_ref, *refs):
+def down(part, order, down_ref, own_ref, other_ref, *refs):
     columns = own_ref.shape[2]
     gate = own_ref[0] + other_ref[0]
     up = own_ref[1] + other_ref[1]
     hidden = (gate / (1.0 + jnp.exp(-gate)) * up).astype(jnp.bfloat16)
     width = down_ref.shape[1]
     tile = min(TILE, width)
-    if last:
+    if order:
         *totals, routes_ref, gates_ref, out_ref, terms_ref = refs
-        terms_ref[...] = spread(routes_ref[...], gates_ref[...], terms_ref.shape[0])
+        terms_ref[...] = spread(routes_ref[...], gates_ref[...], order)
     else:
         *totals, out_ref = refs
     for start in range(0, width, tile):
@@ -135,8 +143,13 @@
     routes_t, gates_t = routes.T, gate_weights.T
     n = lax.axis_size("expert")
     copies = n // FLIGHT
+    order = ORDERS.get(n, tuple(range(FLIGHT)))
+    exchange = functools.partial(
+        lax.all_to_all, axis_name="expert", split_axis=0, concat_axis=0, tiled=True,
+        axis_index_groups=[list(order)] if copies == 1 else None,
+    )
     outgoing = pl.pallas_call(
-        pack,
+        functools.partial(pack, order),
         out_shape=jax.ShapeDtypeStruct((FLIGHT, CAP, width), moe_in.dtype),
         in_specs=[pl.BlockSpec(memory_space=pltpu.HBM)] * 2,
         out_specs=VMEM,
@@ -157,7 +170,7 @@
         outgoing = jnp.broadcast_to(outgoing[:, None], (FLIGHT, copies, CAP, width)).reshape(
             n, CAP, width
         )
-    arrived = lax.all_to_all(outgoing, "expert", split_axis=0, concat_axis=0, tiled=True)
+    arrived = exchange(outgoing)
     columns = w_gate.shape[1]
     parts = 2 if columns % (2 * LANES) == 0 else 1
     cores = lax.axis_size("head")
@@ -178,14 +191,14 @@
     for part in range(parts - 1):
         totals = (
             call(
-                functools.partial(down, part, False),
+                functools.partial(down, part, ()),
                 jax.ShapeDtypeStruct((n * CAP, width), jnp.float32),
                 near_down, own[part], other[part], *totals,
                 flops=2 * n * CAP * w_down.size // parts,
             ),
         )
     partial_out, terms = call(
-        functools.partial(down, parts - 1, True),
+        functools.partial(down, parts - 1, order),
         (
             jax.ShapeDtypeStruct((n, CAP, width), moe_in.dtype),
             jax.ShapeDtypeStruct((FLIGHT * CAP, 3 * rows), jnp.bfloat16),
@@ -193,7 +206,7 @@
         near_down, own[-1], other[-1], *totals, routes_t, gates_t,
         flops=2 * n * CAP * w_down.size // parts,
     )
-    returned = lax.all_to_all(partial_out, "expert", split_axis=0, concat_axis=0, tiled=True)
+    returned = exchange(partial_out)
     if copies > 1:
         returned = jnp.sum(
             returned.reshape(FLIGHT, copies, CAP, width).astype(jnp.float32), axis=1

time: 34 us -> 31.2 us (0.918)
  blocking collectives: 24.2 us -> 21.3 us
    all_to_all x2, blocking collectives: 24.2 us -> 21.3 us  [the longest x1 12.6 us: per_device(): arrived = exchange(outgoing)]
  transfers between devices with their start and end apart: 2 -> 2, of which waited for: 0 -> 0; matrix products, arithmetic and copies ran while one was open for 0% -> 0% of each run, Pallas kernels for 9% -> 10%
where the time goes in v4:
time: 31.2 us; the launch traced here: 31 us
  blocking collectives  21.3 us (68%)
  Pallas kernels  8.18 us (26%)
  local copies, waits for them, and re-layouts  0.94 us (3%)
  starting transfers between devices  0.52 us (2%)
    all_to_all x1, blocking collectives, per_device(): arrived = exchange(outgoing)  12.6 us
    all_to_all x1, blocking collectives, per_device(): returned = exchange(partial_out)  8.72 us
    pallas_call x5, Pallas kernels, call(): pl.pallas_call(kernel, out_shape=out_shape, in_specs=[VMEM] * len(operand...  7.02 us
    pallas_call x1, Pallas kernels, per_device(): pl.pallas_call(functools.partial(pack, order), out_shape=jax.ShapeDtypeSt...  1.16 us
    unnamed x16, local copies, waits for them, and re-layouts  0.94 us
  transfers between devices with their start and end apart: 2, of which 0 were waited for; matrix products, arithmetic and copies ran while one was open for 0% of the time, Pallas kernels for 10%

profile of v4, /device:TPU:0, one launch (start us, length us, event | category | flops | bytes accessed | tf_op | source)
XLA Modules:
  0.0 31.0 jit_solution(7160838466507197418)
XLA Ops:
  0.0 0.0 copy-start
  0.0 0.0 copy-start.1
  0.0 1.2 %pack.1 = bf16[8,2,3584]{2,1,0:T(2,128)(2,1)S(1)} custom-call(s32[2,8]{1,0:T(2,128)} %bitcast.4, bf16[8,3584]{1,0:T(8,128)(2,1)} %rows_hbm.1), custom_call_target="tpu_custom_call" | custom-call | flops 13212057600 | tf_op jit(solution)/shard_map/pack/pallas_call | solution.py:151
  1.2 12.6 %all_to_all.10.rows_ref = bf16[8,2,3584]{2,1,0:T(2,128)(2,1)S(1)} all-to-all(bf16[8,2,3584]{2,1,0:T(2,128)(2,1)S(1)} %pack.1), channel_id=1, replica_groups={{8,4,14,12,0,2,6,10},{9,5,15,13,1,3,7,11},{24,20,30,28,16,18,22,26},{25..., dimensions={0} | all-to-all | bytes 229376 | tf_op jit(solution)/shard_map/all_to_all | solution.py:173
  13.8 0.0 copy-done
  13.8 0.0 copy-done.1
  13.8 0.0 slice-start
  13.8 0.0 slice-start.1
  13.8 2.0 %gate_up.3.own_ref = f32[2,16,1024]{2,1,0:T(8,128)S(1)} custom-call(bf16[8,2,3584]{2,1,0:T(2,128)(2,1)S(1)} %all_to_all.10.rows_ref, bf16[3584,2048]{1,0:T(8,128)(2,1)S(1)} %copy-done, bf16[3584,2048]{1,0:T(8,128)(2,1)S(1)} %copy-done.1), custom_call_target="tpu_custom_call" | custom-call | flops 234881024 | tf_op jit(solution)/shard_map/gate_up/pallas_call | solution.py:29
  15.8 0.0 collective-permute-start.1
  15.8 2.0 %gate_up.2.own_ref = f32[2,16,1024]{2,1,0:T(8,128)S(1)} custom-call(bf16[8,2,3584]{2,1,0:T(2,128)(2,1)S(1)} %all_to_all.10.rows_ref, bf16[3584,2048]{1,0:T(8,128)(2,1)S(1)} %copy-done, bf16[3584,2048]{1,0:T(8,128)(2,1)S(1)} %copy-done.1), custom_call_target="tpu_custom_call" | custom-call | flops 234881024 | tf_op jit(solution)/shard_map/gate_up/pallas_call | solution.py:29
  17.8 0.5 %collective-permute-start = (f32[2,16,1024]{2,1,0:T(8,128)S(1)}, f32[2,16,1024]{2,1,0:T(8,128)S(1)}, u32[]{:S(2)}, u32[]{:S(2)}) collective-permute-start(f32[2,16,1024]{2,1,0:T(8,128)S(1)} %gate_up.2.own_ref), channel_id=1, source_target_pairs={{0,1},{1,0},{2,3},{3,2},{4,5},{5,4},{6,7},{7,6},{8,9},{9,8},{10,11... | collective-permute-start | bytes 393224 | tf_op jit(solution)/shard_map/ppermute | solution.py:189
  18.3 0.0 collective-permute-done.1.other_ref
  18.3 0.0 slice-done
  18.3 0.0 slice-done.1
  18.3 0.3 slice-done.2
  18.6 0.6 %slice-done.3 = s8[2097152]{0:T(1024)(128)(4,1)S(1)} async-done(((s8[14680064]{0:T(1024)(128)(4,1)}), s8[2097152]{0:T(1024)(128)(4,1)S(1)}, s32[]{:S(2)}) %slice-start.3) | async-done | bytes 2097176
  19.2 1.1 %down.2.refs_0_ = f32[16,3584]{1,0:T(8,128)S(1)} custom-call(bf16[2048,3584]{1,0:T(8,128)(2,1)S(1)} %bitcast.3, f32[2,16,1024]{2,1,0:T(8,128)S(1)} %gate_up.3.own_ref, f32[2,16,1024]{2,1,0:T(8,128)S(1)} %collective-permute-done.1.other_ref), custom_call_target="tpu_custom_call" | custom-call | flops 117440512 | tf_op jit(solution)/shard_map/down/pallas_call | solution.py:29
  20.3 0.0 collective-permute-done.other_ref
  20.3 0.0 copy-done.2
  20.3 0.0 copy-done.3
  20.3 1.1 %down.3 = (bf16[8,2,3584]{2,1,0:T(2,128)(2,1)S(1)}, bf16[16,24]{1,0:T(8,128)(2,1)S(1)}) custom-call(bf16[2048,3584]{1,0:T(8,128)(2,1)S(1)} %bitcast.3, f32[2,16,1024]{2,1,0:T(8,128)S(1)} %gate_up.2.own_ref, f32[2,16,1024]{2,1,0:T(8,128)S(1)} %collective-permute-done.other_ref, f32[16,3584]{1,0:T(8,128)S(1)} %down.2.refs_0_, s32[2,8]{1,0:T(2,128)S(1)} %bitcast.5, ...), custom_call_target="tpu_custom_call" | custom-call | flops 117440512 | tf_op jit(solution)/shard_map/down/pallas_call | solution.py:29
  21.4 8.7 %all_to_all.11.slots_ref = bf16[8,2,3584]{2,1,0:T(2,128)(2,1)S(1)} all-to-all(bf16[8,2,3584]{2,1,0:T(2,128)(2,1)S(1)} %get-tuple-element.8), channel_id=1, replica_groups={{8,4,14,12,0,2,6,10},{9,5,15,13,1,3,7,11},{24,20,30,28,16,18,22,26},{25..., dimensions={0} | all-to-all | bytes 229376 | tf_op jit(solution)/shard_map/all_to_all | solution.py:209
  30.1 0.9 %unpack.1 = bf16[8,3584]{1,0:T(8,128)(2,1)} custom-call(bf16[16,24]{1,0:T(8,128)(2,1)S(1)} %get-tuple-element.7.terms_ref, bf16[8,2,3584]{2,1,0:T(2,128)(2,1)S(1)} %all_to_all.11.slots_ref), custom_call_target="tpu_custom_call" | custom-call | tf_op jit(solution)/shard_map/unpack/pallas_call | solution.py:29
  (5 shorter events, 0.0 us)
Async XLA Ops:
  0.0 13.8 %copy-start = (bf16[3584,2048]{1,0:T(8,128)(2,1)S(1)}, bf16[3584,2048]{1,0:T(8,128)(2,1)}, u32[]{:S(2)}) copy-start(bf16[3584,2048]{1,0:T(8,128)(2,1)} %gate_ref.3) | copy-start | bytes 44040196
  0.0 13.8 %copy-start.1 = (bf16[3584,2048]{1,0:T(8,128)(2,1)S(1)}, bf16[3584,2048]{1,0:T(8,128)(2,1)}, u32[]{:S(2)}) copy-start(bf16[3584,2048]{1,0:T(8,128)(2,1)} %up_ref.3) | copy-start | bytes 44040196
  13.8 4.6 %slice-start = ((s8[14680064]{0:T(1024)(128)(4,1)}), s8[4194304]{0:T(1024)(128)(4,1)S(1)}, s32[]{:S(2)}) async-start(s8[14680064]{0:T(1024)(128)(4,1)} %bitcast.2), calls=%async_computation.2 | async-start | bytes 8388608
  13.8 4.6 %slice-start.1 = ((s8[14680064]{0:T(1024)(128)(4,1)}), s8[4194304]{0:T(1024)(128)(4,1)S(1)}, s32[]{:S(2)}) async-start(s8[14680064]{0:T(1024)(128)(4,1)} %bitcast.2), calls=%async_computation.3 | async-start | bytes 8388608
  15.8 2.9 %slice-start.2 = ((s8[14680064]{0:T(1024)(128)(4,1)}), s8[4194304]{0:T(1024)(128)(4,1)S(1)}, s32[]{:S(2)}) async-start(s8[14680064]{0:T(1024)(128)(4,1)} %bitcast.2), calls=%async_computation.4 | async-start | bytes 8388608
  15.8 3.5 %slice-start.3 = ((s8[14680064]{0:T(1024)(128)(4,1)}), s8[2097152]{0:T(1024)(128)(4,1)S(1)}, s32[]{:S(2)}) async-start(s8[14680064]{0:T(1024)(128)(4,1)} %bitcast.2), calls=%async_computation.5 | async-start | bytes 4194304
  15.8 2.5 %collective-permute-start.1 = (f32[2,16,1024]{2,1,0:T(8,128)S(1)}, f32[2,16,1024]{2,1,0:T(8,128)S(1)}, u32[]{:S(2)}, u32[]{:S(2)}) collective-permute-start(f32[2,16,1024]{2,1,0:T(8,128)S(1)} %gate_up.3.own_ref), channel_id=1, source_target_pairs={{0,1},{1,0},{2,3},{3,2},{4,5},{5,4},{6,7},{7,6},{8,9},{9,8},{10,11... | collective-permute-start | bytes 393224 | tf_op jit(solution)/shard_map/ppermute | solution.py:189
  17.8 2.5 %copy-start.2 = (s32[8,2]{0,1:T(2,128)S(1)}, s32[8,2]{0,1:T(2,128)}, u32[]{:S(2)}) copy-start(s32[8,2]{0,1:T(2,128)} %param.7) | copy-start | bytes 196
  17.8 2.5 %copy-start.3 = (f32[8,2]{0,1:T(2,128)S(1)}, f32[8,2]{0,1:T(2,128)}, u32[]{:S(2)}) copy-start(f32[8,2]{0,1:T(2,128)} %param.8) | copy-start | bytes 196
  17.8 2.5 %collective-permute-start = (f32[2,16,1024]{2,1,0:T(8,128)S(1)}, f32[2,16,1024]{2,1,0:T(8,128)S(1)}, u32[]{:S(2)}, u32[]{:S(2)}) collective-permute-start(f32[2,16,1024]{2,1,0:T(8,128)S(1)} %gate_up.2.own_ref), channel_id=1, source_target_pairs={{0,1},{1,0},{2,3},{3,2},{4,5},{5,4},{6,7},{7,6},{8,9},{9,8},{10,11... | collective-permute-start | bytes 393224 | tf_op jit(solution)/shard_map/ppermute | solution.py:189

commit v5 on v4

--- a/solution.py
+++ b/solution.py
@@ -11,8 +11,8 @@
 CAP = 2
 TILE = 512
 LANES = 128
-ORDERS = {8: (4, 2, 7, 6, 0, 1, 3, 5)}
-AHEAD = 300
+ORDERS = {8: (5, 0, 2, 7, 1, 3, 6, 4)}
+AHEAD = 450
 SMALL = pltpu.CompilerParams(vmem_limit_bytes=4 << 20)
 VMEM = pl.BlockSpec(memory_space=pltpu.VMEM)
 
@@ -76,15 +76,16 @@
     out_ref[...] = packed.reshape(out_ref.shape)
 
 
-def gate_up(part, rows_ref, gate_ref, up_ref, out_ref):
+def project(blocks, *refs):
+    *weights, rows_ref, out_ref = refs
     columns = out_ref.shape[2]
     tile = min(TILE, columns)
     rows = rows_ref[...].reshape(-1, rows_ref.shape[-1])
-    for start in range(0, columns, tile):
-        for k, weights in enumerate((gate_ref, up_ref)):
-            out_ref[k, :, start : start + tile] = jnp.dot(
+    for block, (which, part) in enumerate(blocks):
+        for start in range(0, columns, tile):
+            out_ref[block, :, start : start + tile] = jnp.dot(
                 rows,
-                weights[:, part * columns + start : part * columns + start + tile],
+                weights[which][:, part * columns + start : part * columns + start + tile],
                 preferred_element_type=jnp.float32,
             )
 
@@ -102,10 +103,11 @@
     return jnp.concatenate(terms, axis=1)
 
 
-def down(part, order, down_ref, own_ref, other_ref, *refs):
-    columns = own_ref.shape[2]
-    gate = own_ref[0] + other_ref[0]
-    up = own_ref[1] + other_ref[1]
+def down(part, order, gate_block, up_block, down_ref, *refs):
+    gate_ref, gate_other, up_ref, up_other, *refs = refs
+    columns = up_ref.shape[2]
+    gate = gate_ref[gate_block] + gate_other[gate_block]
+    up = up_ref[up_block] + up_other[up_block]
     hidden = (gate / (1.0 + jnp.exp(-gate)) * up).astype(jnp.bfloat16)
     width = down_ref.shape[1]
     tile = min(TILE, width)
@@ -176,34 +178,36 @@
     cores = lax.axis_size("head")
     swap = [(i, (i + 1) % cores) for i in range(cores)]
     near_gate, near_up, near_down = near(w_gate), near(w_up), near(w_down)
-    own, other = [], []
-    for part in range(parts):
-        own.append(
-            call(
-                functools.partial(gate_up, part),
-                jax.ShapeDtypeStruct((2, n * CAP, columns // parts), jnp.float32),
-                arrived, near_gate, near_up,
-                flops=4 * n * CAP * w_gate.size // parts,
-            )
-        )
-        other.append(lax.ppermute(own[-1], "head", swap))
+
+    def swapped(blocks, *weights):
+        product = call(
+            functools.partial(project, blocks),
+            jax.ShapeDtypeStruct((len(blocks), n * CAP, columns // parts), jnp.float32),
+            *weights, arrived,
+            flops=2 * n * CAP * len(blocks) * w_gate.size // parts,
+        )
+        return product, lax.ppermute(product, "head", swap)
+
+    first = swapped([(1, part) for part in range(parts)] + [(0, 0)], near_up, near_gate)
+    later = [swapped([(0, part)], near_up) for part in range(1, parts)]
+    places = [(first, parts)] + [(pair, 0) for pair in later]
     totals = ()
     for part in range(parts - 1):
         totals = (
             call(
-                functools.partial(down, part, ()),
+                functools.partial(down, part, (), part, places[part][1]),
                 jax.ShapeDtypeStruct((n * CAP, width), jnp.float32),
-                near_down, own[part], other[part], *totals,
+                near_down, *first, *places[part][0], *totals,
                 flops=2 * n * CAP * w_down.size // parts,
             ),
         )
     partial_out, terms = call(
-        functools.partial(down, parts - 1, order),
+        functools.partial(down, parts - 1, order, parts - 1, places[-1][1]),
         (
             jax.ShapeDtypeStruct((n, CAP, width), moe_in.dtype),
             jax.ShapeDtypeStruct((FLIGHT * CAP, 3 * rows), jnp.bfloat16),
         ),
-        near_down, own[-1], other[-1], *totals, routes_t, gates_t,
+        near_down, *first, *places[-1][0], *totals, routes_t, gates_t,
         flops=2 * n * CAP * w_down.size // parts,
     )
     returned = exchange(partial_out)

time: 31.2 us -> 30.1 us (0.965)
  blocking collectives: 21.3 us -> 20.2 us
    all_to_all x1, blocking collectives: 12.6 us -> 11.4 us  [per_device(): arrived = exchange(outgoing)]
  transfers between devices with their start and end apart: 2 -> 2, of which waited for: 0 -> 0; matrix products, arithmetic and copies ran while one was open for 0% -> 0% of each run, Pallas kernels for 10% -> 7%
where the time goes in v5:
time: 30.1 us; the launch traced here: 29.9 us
  blocking collectives  20.2 us (67%)
  Pallas kernels  8.16 us (27%)
  local copies, waits for them, and re-layouts  0.91 us (3%)
  starting transfers between devices  0.57 us (2%)
    all_to_all x1, blocking collectives, per_device(): arrived = exchange(outgoing)  11.4 us
    all_to_all x1, blocking collectives, per_device(): returned = exchange(partial_out)  8.79 us
    pallas_call x5, Pallas kernels, call(): pl.pallas_call(kernel, out_shape=out_shape, in_specs=[VMEM] * len(operand...  7 us
    pallas_call x1, Pallas kernels, per_device(): pl.pallas_call(functools.partial(pack, order), out_shape=jax.ShapeDtypeSt...  1.16 us
    unnamed x16, local copies, waits for them, and re-layouts  0.91 us
  transfers between devices with their start and end apart: 2, of which 0 were waited for; matrix products, arithmetic and copies ran while one was open for 0% of the time, Pallas kernels for 7%

profile of v5, /device:TPU:0, one launch (start us, length us, event | category | flops | bytes accessed | tf_op | source)
XLA Modules:
  0.0 29.9 jit_solution(8881461928380011080)
XLA Ops:
  0.0 0.0 copy-start
  0.0 0.0 copy-start.1
  0.0 1.2 %pack.1 = bf16[8,2,3584]{2,1,0:T(2,128)(2,1)S(1)} custom-call(s32[2,8]{1,0:T(2,128)} %bitcast.4, bf16[8,3584]{1,0:T(8,128)(2,1)} %rows_hbm.1), custom_call_target="tpu_custom_call" | custom-call | flops 19818086400 | tf_op jit(solution)/shard_map/pack/pallas_call | solution.py:153
  1.2 11.4 %all_to_all.10.refs_2_.refs_1_ = bf16[8,2,3584]{2,1,0:T(2,128)(2,1)S(1)} all-to-all(bf16[8,2,3584]{2,1,0:T(2,128)(2,1)S(1)} %pack.1), channel_id=1, replica_groups={{10,0,4,14,2,6,12,8},{11,1,5,15,3,7,13,9},{26,16,20,30,18,22,28,24},{27..., dimensions={0} | all-to-all | bytes 229376 | tf_op jit(solution)/shard_map/all_to_all | solution.py:175
  12.6 0.0 copy-done
  12.6 0.0 copy-done.1
  12.6 0.0 slice-start
  12.6 0.0 slice-start.2
  12.6 2.9 %project.2.refs_0_.refs_2_ = f32[3,16,1024]{2,1,0:T(8,128)S(1)} custom-call(bf16[3584,2048]{1,0:T(8,128)(2,1)S(1)} %copy-done, bf16[3584,2048]{1,0:T(8,128)(2,1)S(1)} %copy-done.1, bf16[8,2,3584]{2,1,0:T(2,128)(2,1)S(1)} %all_to_all.10.refs_2_.refs_1_), custom_call_target="tpu_custom_call" | custom-call | flops 352321536 | tf_op jit(solution)/shard_map/project/pallas_call | solution.py:29
  15.5 0.1 collective-permute-start
  15.6 1.1 %project.3.refs_2_ = f32[1,16,1024]{2,1,0:T(8,128)S(1)} custom-call(bf16[3584,2048]{1,0:T(8,128)(2,1)S(1)} %copy-done, bf16[8,2,3584]{2,1,0:T(2,128)(2,1)S(1)} %all_to_all.10.refs_2_.refs_1_), custom_call_target="tpu_custom_call" | custom-call | flops 117440512 | tf_op jit(solution)/shard_map/project/pallas_call | solution.py:29
  16.7 0.5 %collective-permute-start.1 = (f32[1,16,1024]{2,1,0:T(8,128)S(1)}, f32[1,16,1024]{2,1,0:T(8,128)S(1)}, u32[]{:S(2)}, u32[]{:S(2)}) collective-permute-start(f32[1,16,1024]{2,1,0:T(8,128)S(1)} %project.3.refs_2_), channel_id=1, source_target_pairs={{0,1},{1,0},{2,3},{3,2},{4,5},{5,4},{6,7},{7,6},{8,9},{9,8},{10,11... | collective-permute-start | bytes 196616 | tf_op jit(solution)/shard_map/ppermute | solution.py:189
  17.2 0.0 collective-permute-done.refs_1_.refs_3_
  17.2 0.0 slice-done
  17.2 0.0 slice-done.1
  17.2 0.1 slice-done.2
  17.2 0.8 %slice-done.3 = s8[2097152]{0:T(1024)(128)(4,1)S(1)} async-done(((s8[14680064]{0:T(1024)(128)(4,1)}), s8[2097152]{0:T(1024)(128)(4,1)S(1)}, s32[]{:S(2)}) %slice-start.3) | async-done | bytes 2097176
  18.1 1.1 %down.2.refs_4_ = f32[16,3584]{1,0:T(8,128)S(1)} custom-call(bf16[2048,3584]{1,0:T(8,128)(2,1)S(1)} %bitcast.3, f32[3,16,1024]{2,1,0:T(8,128)S(1)} %project.2.refs_0_.refs_2_, f32[3,16,1024]{2,1,0:T(8,128)S(1)} %collective-permute-done.refs_1_.refs_3_, f32[3,16,1024]{2,1,0:T(8,128)S(1)} %project.2.refs_0_.refs_2_, ...), custom_call_target="tpu_custom_call" | custom-call | flops 117440512 | tf_op jit(solution)/shard_map/down/pallas_call | solution.py:29
  19.1 0.0 collective-permute-done.1.refs_3_
  19.1 0.0 copy-done.2
  19.1 0.0 copy-done.3
  19.1 1.1 %down.3 = (bf16[8,2,3584]{2,1,0:T(2,128)(2,1)S(1)}, bf16[16,24]{1,0:T(8,128)(2,1)S(1)}) custom-call(bf16[2048,3584]{1,0:T(8,128)(2,1)S(1)} %bitcast.3, f32[3,16,1024]{2,1,0:T(8,128)S(1)} %project.2.refs_0_.refs_2_, f32[3,16,1024]{2,1,0:T(8,128)S(1)} %collective-permute-done.refs_1_.refs_3_, f32[1,16,1024]{2,1,0:T(8,128)S(1)} %project.3.refs_2_, ...), custom_call_target="tpu_custom_call" | custom-call | flops 117440512 | tf_op jit(solution)/shard_map/down/pallas_call | solution.py:29
  20.2 8.8 %all_to_all.11.slots_ref = bf16[8,2,3584]{2,1,0:T(2,128)(2,1)S(1)} all-to-all(bf16[8,2,3584]{2,1,0:T(2,128)(2,1)S(1)} %get-tuple-element.8), channel_id=1, replica_groups={{10,0,4,14,2,6,12,8},{11,1,5,15,3,7,13,9},{26,16,20,30,18,22,28,24},{27..., dimensions={0} | all-to-all | bytes 229376 | tf_op jit(solution)/shard_map/all_to_all | solution.py:213
  29.0 0.9 %unpack.1 = bf16[8,3584]{1,0:T(8,128)(2,1)} custom-call(bf16[16,24]{1,0:T(8,128)(2,1)S(1)} %get-tuple-element.7.terms_ref, bf16[8,2,3584]{2,1,0:T(2,128)(2,1)S(1)} %all_to_all.11.slots_ref), custom_call_target="tpu_custom_call" | custom-call | tf_op jit(solution)/shard_map/unpack/pallas_call | solution.py:29
  (5 shorter events, 0.0 us)
Async XLA Ops:
  0.0 12.6 %copy-start = (bf16[3584,2048]{1,0:T(8,128)(2,1)S(1)}, bf16[3584,2048]{1,0:T(8,128)(2,1)}, u32[]{:S(2)}) copy-start(bf16[3584,2048]{1,0:T(8,128)(2,1)} %refs_0_.3) | copy-start | bytes 44040196
  0.0 12.6 %copy-start.1 = (bf16[3584,2048]{1,0:T(8,128)(2,1)S(1)}, bf16[3584,2048]{1,0:T(8,128)(2,1)}, u32[]{:S(2)}) copy-start(bf16[3584,2048]{1,0:T(8,128)(2,1)} %refs_1_.1) | copy-start | bytes 44040196
  12.6 4.6 %slice-start = ((s8[14680064]{0:T(1024)(128)(4,1)}), s8[4194304]{0:T(1024)(128)(4,1)S(1)}, s32[]{:S(2)}) async-start(s8[14680064]{0:T(1024)(128)(4,1)} %bitcast.2), calls=%async_computation.2 | async-start | bytes 8388608
  12.6 4.6 %slice-start.1 = ((s8[14680064]{0:T(1024)(128)(4,1)}), s8[4194304]{0:T(1024)(128)(4,1)S(1)}, s32[]{:S(2)}) async-start(s8[14680064]{0:T(1024)(128)(4,1)} %bitcast.2), calls=%async_computation.3 | async-start | bytes 8388608
  12.6 4.7 %slice-start.2 = ((s8[14680064]{0:T(1024)(128)(4,1)}), s8[4194304]{0:T(1024)(128)(4,1)S(1)}, s32[]{:S(2)}) async-start(s8[14680064]{0:T(1024)(128)(4,1)} %bitcast.2), calls=%async_computation.4 | async-start | bytes 8388608
  15.5 2.5 %slice-start.3 = ((s8[14680064]{0:T(1024)(128)(4,1)}), s8[2097152]{0:T(1024)(128)(4,1)S(1)}, s32[]{:S(2)}) async-start(s8[14680064]{0:T(1024)(128)(4,1)} %bitcast.2), calls=%async_computation.5 | async-start | bytes 4194304
  15.5 3.6 %copy-start.2 = (s32[8,2]{0,1:T(2,128)S(1)}, s32[8,2]{0,1:T(2,128)}, u32[]{:S(2)}) copy-start(s32[8,2]{0,1:T(2,128)} %param.7) | copy-start | bytes 196
  15.5 3.6 %copy-start.3 = (f32[8,2]{0,1:T(2,128)S(1)}, f32[8,2]{0,1:T(2,128)}, u32[]{:S(2)}) copy-start(f32[8,2]{0,1:T(2,128)} %param.8) | copy-start | bytes 196
  15.5 1.6 %collective-permute-start = (f32[3,16,1024]{2,1,0:T(8,128)S(1)}, f32[3,16,1024]{2,1,0:T(8,128)S(1)}, u32[]{:S(2)}, u32[]{:S(2)}) collective-permute-start(f32[3,16,1024]{2,1,0:T(8,128)S(1)} %project.2.refs_0_.refs_2_), channel_id=1, source_target_pairs={{0,1},{1,0},{2,3},{3,2},{4,5},{5,4},{6,7},{7,6},{8,9},{9,8},{10,11... | collective-permute-start | bytes 589832 | tf_op jit(solution)/shard_map/ppermute | solution.py:189
  16.7 2.5 %collective-permute-start.1 = (f32[1,16,1024]{2,1,0:T(8,128)S(1)}, f32[1,16,1024]{2,1,0:T(8,128)S(1)}, u32[]{:S(2)}, u32[]{:S(2)}) collective-permute-start(f32[1,16,1024]{2,1,0:T(8,128)S(1)} %project.3.refs_2_), channel_id=1, source_target_pairs={{0,1},{1,0},{2,3},{3,2},{4,5},{5,4},{6,7},{7,6},{8,9},{9,8},{10,11... | collective-permute-start | bytes 196616 | tf_op jit(solution)/shard_map/ppermute | solution.py:189

commit v6 on v5

--- a/solution.py
+++ b/solution.py
@@ -96,11 +96,11 @@
     weight = jnp.zeros(place.shape, jnp.float32)
     for k in range(routes.shape[0]):
         weight += jnp.where(routes[k : k + 1, :] == expert, gates[k : k + 1, :], 0.0)
-    rest, terms = place * weight, []
+    rest, terms = (place * weight).T, []
     for _ in range(3):
         terms.append(rest.astype(jnp.bfloat16))
         rest = rest - terms[-1].astype(jnp.float32)
-    return jnp.concatenate(terms, axis=1)
+    return jnp.concatenate(terms, axis=0)
 
 
 def down(part, order, gate_block, up_block, down_ref, *refs):
@@ -130,14 +130,20 @@
 
 def unpack(terms_ref, slots_ref, out_ref):
     experts, cap, width = slots_ref.shape
-    sums = lax.dot_general(
-        terms_ref[...],
-        slots_ref[...].astype(jnp.bfloat16).reshape(experts * cap, width),
-        (((0,), (0,)), ((), ())),
-        preferred_element_type=jnp.float32,
-    )
     rows = out_ref.shape[0]
-    out_ref[...] = (sums[:rows] + sums[rows : 2 * rows] + sums[2 * rows :]).astype(out_ref.dtype)
+    slots = slots_ref[...].reshape(experts * cap, width)
+    if slots.dtype == jnp.bfloat16:
+        sums = jnp.dot(terms_ref[...], slots, preferred_element_type=jnp.float32)
+        total = sums[:rows] + sums[rows : 2 * rows] + sums[2 * rows :]
+    else:
+        terms = terms_ref[...].astype(jnp.float32)
+        total = jnp.dot(
+            terms[:rows] + terms[rows : 2 * rows] + terms[2 * rows :],
+            slots,
+            precision=lax.Precision.HIGHEST,
+            preferred_element_type=jnp.float32,
+        )
+    out_ref[...] = total.astype(out_ref.dtype)
 
 
 def per_device(moe_in, routes, gate_weights, w_gate, w_up, w_down):
@@ -205,7 +211,7 @@
         functools.partial(down, parts - 1, order, parts - 1, places[-1][1]),
         (
             jax.ShapeDtypeStruct((n, CAP, width), moe_in.dtype),
-            jax.ShapeDtypeStruct((FLIGHT * CAP, 3 * rows), jnp.bfloat16),
+            jax.ShapeDtypeStruct((3 * rows, FLIGHT * CAP), jnp.bfloat16),
         ),
         near_down, *first, *places[-1][0], *totals, routes_t, gates_t,
         flops=2 * n * CAP * w_down.size // parts,

time: 30.1 us -> 30 us (level)
  no operation moved by 1% of the time
where the time goes in v6:
time: 30 us; the launch traced here: 29.8 us
  blocking collectives  20.2 us (67%)
  Pallas kernels  8.12 us (27%)
  local copies, waits for them, and re-layouts  0.91 us (3%)
  starting transfers between devices  0.57 us (2%)
    all_to_all x1, blocking collectives, per_device(): arrived = exchange(outgoing)  11.4 us
    all_to_all x1, blocking collectives, per_device(): returned = exchange(partial_out)  8.79 us
    pallas_call x5, Pallas kernels, call(): pl.pallas_call(kernel, out_shape=out_shape, in_specs=[VMEM] * len(operand...  6.96 us
    pallas_call x1, Pallas kernels, per_device(): pl.pallas_call(functools.partial(pack, order), out_shape=jax.ShapeDtypeSt...  1.16 us
    unnamed x16, local copies, waits for them, and re-layouts  0.91 us
  transfers between devices with their start and end apart: 2, of which 0 were waited for; matrix products, arithmetic and copies ran while one was open for 0% of the time, Pallas kernels for 7%

profile of v6, /device:TPU:0, one launch (start us, length us, event | category | flops | bytes accessed | tf_op | source)
XLA Modules:
  0.0 29.8 jit_solution(3766947774856199558)
XLA Ops:
  0.0 0.0 copy-start
  0.0 0.0 copy-start.1
  0.0 1.2 %pack.1 = bf16[8,2,3584]{2,1,0:T(2,128)(2,1)S(1)} custom-call(s32[2,8]{1,0:T(2,128)} %bitcast.4, bf16[8,3584]{1,0:T(8,128)(2,1)} %rows_hbm.1), custom_call_target="tpu_custom_call" | custom-call | flops 19818086400 | tf_op jit(solution)/shard_map/pack/pallas_call | solution.py:159
  1.2 11.4 %all_to_all.10.refs_2_.refs_1_ = bf16[8,2,3584]{2,1,0:T(2,128)(2,1)S(1)} all-to-all(bf16[8,2,3584]{2,1,0:T(2,128)(2,1)S(1)} %pack.1), channel_id=1, replica_groups={{10,0,4,14,2,6,12,8},{11,1,5,15,3,7,13,9},{26,16,20,30,18,22,28,24},{27..., dimensions={0} | all-to-all | bytes 229376 | tf_op jit(solution)/shard_map/all_to_all | solution.py:181
  12.6 0.0 copy-done
  12.6 0.0 copy-done.1
  12.6 0.0 slice-start
  12.6 0.0 slice-start.2
  12.6 2.9 %project.2.refs_0_.refs_2_ = f32[3,16,1024]{2,1,0:T(8,128)S(1)} custom-call(bf16[3584,2048]{1,0:T(8,128)(2,1)S(1)} %copy-done, bf16[3584,2048]{1,0:T(8,128)(2,1)S(1)} %copy-done.1, bf16[8,2,3584]{2,1,0:T(2,128)(2,1)S(1)} %all_to_all.10.refs_2_.refs_1_), custom_call_target="tpu_custom_call" | custom-call | flops 352321536 | tf_op jit(solution)/shard_map/project/pallas_call | solution.py:29
  15.5 0.1 collective-permute-start
  15.6 1.1 %project.3.refs_2_ = f32[1,16,1024]{2,1,0:T(8,128)S(1)} custom-call(bf16[3584,2048]{1,0:T(8,128)(2,1)S(1)} %copy-done, bf16[8,2,3584]{2,1,0:T(2,128)(2,1)S(1)} %all_to_all.10.refs_2_.refs_1_), custom_call_target="tpu_custom_call" | custom-call | flops 117440512 | tf_op jit(solution)/shard_map/project/pallas_call | solution.py:29
  16.7 0.5 %collective-permute-start.1 = (f32[1,16,1024]{2,1,0:T(8,128)S(1)}, f32[1,16,1024]{2,1,0:T(8,128)S(1)}, u32[]{:S(2)}, u32[]{:S(2)}) collective-permute-start(f32[1,16,1024]{2,1,0:T(8,128)S(1)} %project.3.refs_2_), channel_id=1, source_target_pairs={{0,1},{1,0},{2,3},{3,2},{4,5},{5,4},{6,7},{7,6},{8,9},{9,8},{10,11... | collective-permute-start | bytes 196616 | tf_op jit(solution)/shard_map/ppermute | solution.py:195
  17.2 0.0 collective-permute-done.refs_1_.refs_3_
  17.2 0.0 slice-done
  17.2 0.0 slice-done.1
  17.2 0.1 slice-done.2
  17.2 0.8 %slice-done.3 = s8[2097152]{0:T(1024)(128)(4,1)S(1)} async-done(((s8[14680064]{0:T(1024)(128)(4,1)}), s8[2097152]{0:T(1024)(128)(4,1)S(1)}, s32[]{:S(2)}) %slice-start.3) | async-done | bytes 2097176
  18.1 1.1 %down.2.refs_4_ = f32[16,3584]{1,0:T(8,128)S(1)} custom-call(bf16[2048,3584]{1,0:T(8,128)(2,1)S(1)} %bitcast.3, f32[3,16,1024]{2,1,0:T(8,128)S(1)} %project.2.refs_0_.refs_2_, f32[3,16,1024]{2,1,0:T(8,128)S(1)} %collective-permute-done.refs_1_.refs_3_, f32[3,16,1024]{2,1,0:T(8,128)S(1)} %project.2.refs_0_.refs_2_, ...), custom_call_target="tpu_custom_call" | custom-call | flops 117440512 | tf_op jit(solution)/shard_map/down/pallas_call | solution.py:29
  19.1 0.0 collective-permute-done.1.refs_3_
  19.1 0.0 copy-done.2
  19.1 0.0 copy-done.3
  19.1 1.1 %down.3 = (bf16[8,2,3584]{2,1,0:T(2,128)(2,1)S(1)}, bf16[24,16]{1,0:T(8,128)(2,1)S(1)}) custom-call(bf16[2048,3584]{1,0:T(8,128)(2,1)S(1)} %bitcast.3, f32[3,16,1024]{2,1,0:T(8,128)S(1)} %project.2.refs_0_.refs_2_, f32[3,16,1024]{2,1,0:T(8,128)S(1)} %collective-permute-done.refs_1_.refs_3_, f32[1,16,1024]{2,1,0:T(8,128)S(1)} %project.3.refs_2_, ...), custom_call_target="tpu_custom_call" | custom-call | flops 117440512 | tf_op jit(solution)/shard_map/down/pallas_call | solution.py:29
  20.2 8.8 %all_to_all.11.slots_ref = bf16[8,2,3584]{2,1,0:T(2,128)(2,1)S(1)} all-to-all(bf16[8,2,3584]{2,1,0:T(2,128)(2,1)S(1)} %get-tuple-element.8), channel_id=1, replica_groups={{10,0,4,14,2,6,12,8},{11,1,5,15,3,7,13,9},{26,16,20,30,18,22,28,24},{27..., dimensions={0} | all-to-all | bytes 229376 | tf_op jit(solution)/shard_map/all_to_all | solution.py:219
  29.0 0.8 %unpack.1 = bf16[8,3584]{1,0:T(8,128)(2,1)} custom-call(bf16[24,16]{1,0:T(8,128)(2,1)S(1)} %get-tuple-element.7.terms_ref, bf16[8,2,3584]{2,1,0:T(2,128)(2,1)S(1)} %all_to_all.11.slots_ref), custom_call_target="tpu_custom_call" | custom-call | tf_op jit(solution)/shard_map/unpack/pallas_call | solution.py:29
  (5 shorter events, 0.0 us)
Async XLA Ops:
  0.0 12.6 %copy-start = (bf16[3584,2048]{1,0:T(8,128)(2,1)S(1)}, bf16[3584,2048]{1,0:T(8,128)(2,1)}, u32[]{:S(2)}) copy-start(bf16[3584,2048]{1,0:T(8,128)(2,1)} %refs_0_.3) | copy-start | bytes 44040196
  0.0 12.6 %copy-start.1 = (bf16[3584,2048]{1,0:T(8,128)(2,1)S(1)}, bf16[3584,2048]{1,0:T(8,128)(2,1)}, u32[]{:S(2)}) copy-start(bf16[3584,2048]{1,0:T(8,128)(2,1)} %refs_1_.1) | copy-start | bytes 44040196
  12.6 4.6 %slice-start = ((s8[14680064]{0:T(1024)(128)(4,1)}), s8[4194304]{0:T(1024)(128)(4,1)S(1)}, s32[]{:S(2)}) async-start(s8[14680064]{0:T(1024)(128)(4,1)} %bitcast.2), calls=%async_computation.2 | async-start | bytes 8388608
  12.6 4.6 %slice-start.1 = ((s8[14680064]{0:T(1024)(128)(4,1)}), s8[4194304]{0:T(1024)(128)(4,1)S(1)}, s32[]{:S(2)}) async-start(s8[14680064]{0:T(1024)(128)(4,1)} %bitcast.2), calls=%async_computation.3 | async-start | bytes 8388608
  12.6 4.7 %slice-start.2 = ((s8[14680064]{0:T(1024)(128)(4,1)}), s8[4194304]{0:T(1024)(128)(4,1)S(1)}, s32[]{:S(2)}) async-start(s8[14680064]{0:T(1024)(128)(4,1)} %bitcast.2), calls=%async_computation.4 | async-start | bytes 8388608
  15.5 2.5 %slice-start.3 = ((s8[14680064]{0:T(1024)(128)(4,1)}), s8[2097152]{0:T(1024)(128)(4,1)S(1)}, s32[]{:S(2)}) async-start(s8[14680064]{0:T(1024)(128)(4,1)} %bitcast.2), calls=%async_computation.5 | async-start | bytes 4194304
  15.5 3.6 %copy-start.2 = (s32[8,2]{0,1:T(2,128)S(1)}, s32[8,2]{0,1:T(2,128)}, u32[]{:S(2)}) copy-start(s32[8,2]{0,1:T(2,128)} %param.7) | copy-start | bytes 196
  15.5 3.6 %copy-start.3 = (f32[8,2]{0,1:T(2,128)S(1)}, f32[8,2]{0,1:T(2,128)}, u32[]{:S(2)}) copy-start(f32[8,2]{0,1:T(2,128)} %param.8) | copy-start | bytes 196
  15.5 1.6 %collective-permute-start = (f32[3,16,1024]{2,1,0:T(8,128)S(1)}, f32[3,16,1024]{2,1,0:T(8,128)S(1)}, u32[]{:S(2)}, u32[]{:S(2)}) collective-permute-start(f32[3,16,1024]{2,1,0:T(8,128)S(1)} %project.2.refs_0_.refs_2_), channel_id=1, source_target_pairs={{0,1},{1,0},{2,3},{3,2},{4,5},{5,4},{6,7},{7,6},{8,9},{9,8},{10,11... | collective-permute-start | bytes 589832 | tf_op jit(solution)/shard_map/ppermute | solution.py:195
  16.7 2.5 %collective-permute-start.1 = (f32[1,16,1024]{2,1,0:T(8,128)S(1)}, f32[1,16,1024]{2,1,0:T(8,128)S(1)}, u32[]{:S(2)}, u32[]{:S(2)}) collective-permute-start(f32[1,16,1024]{2,1,0:T(8,128)S(1)} %project.3.refs_2_), channel_id=1, source_target_pairs={{0,1},{1,0},{2,3},{3,2},{4,5},{5,4},{6,7},{7,6},{8,9},{9,8},{10,11... | collective-permute-start | bytes 196616 | tf_op jit(solution)/shard_map/ppermute | solution.py:195

commit v7 on v6

--- a/solution.py
+++ b/solution.py
@@ -103,8 +103,8 @@
     return jnp.concatenate(terms, axis=0)
 
 
-def down(part, order, gate_block, up_block, down_ref, *refs):
-    gate_ref, gate_other, up_ref, up_other, *refs = refs
+def down(part, order, gate_block, up_block, gate_ref, down_ref, *refs):
+    gate_other, up_ref, up_other, *refs = refs
     columns = up_ref.shape[2]
     gate = gate_ref[gate_block] + gate_other[gate_block]
     up = up_ref[up_block] + up_other[up_block]
@@ -195,7 +195,7 @@
         return product, lax.ppermute(product, "head", swap)
 
     first = swapped([(1, part) for part in range(parts)] + [(0, 0)], near_up, near_gate)
-    later = [swapped([(0, part)], near_up) for part in range(1, parts)]
+    later = [swapped([(0, part)], near_up, near_down) for part in range(1, parts)]
     places = [(first, parts)] + [(pair, 0) for pair in later]
     totals = ()
     for part in range(parts - 1):
@@ -203,7 +203,7 @@
             call(
                 functools.partial(down, part, (), part, places[part][1]),
                 jax.ShapeDtypeStruct((n * CAP, width), jnp.float32),
-                near_down, *first, *places[part][0], *totals,
+                first[0], near_down, first[1], *places[part][0], *totals,
                 flops=2 * n * CAP * w_down.size // parts,
             ),
         )
@@ -213,7 +213,7 @@
             jax.ShapeDtypeStruct((n, CAP, width), moe_in.dtype),
             jax.ShapeDtypeStruct((3 * rows, FLIGHT * CAP), jnp.bfloat16),
         ),
-        near_down, *first, *places[-1][0], *totals, routes_t, gates_t,
+        first[0], near_down, first[1], *places[-1][0], *totals, routes_t, gates_t,
         flops=2 * n * CAP * w_down.size // parts,
     )
     returned = exchange(partial_out)

time: 30 us -> 29.7 us (0.990)
  local copies, waits for them, and re-layouts: 0.91 us -> 0.05 us
  blocking collectives: 20.2 us -> 20.8 us
    unnamed x16, local copies, waits for them, and re-layouts: 0.91 us -> 0.05 us
    all_to_all x1, blocking collectives: 8.79 us -> 9.35 us  [per_device(): returned = exchange(partial_out)]
where the time goes in v7:
time: 29.7 us; the launch traced here: 29.5 us
  blocking collectives  20.8 us (70%)
  Pallas kernels  8.12 us (27%)
  starting transfers between devices  0.51 us (2%)
    all_to_all x1, blocking collectives, per_device(): arrived = exchange(outgoing)  11.4 us
    all_to_all x1, blocking collectives, per_device(): returned = exchange(partial_out)  9.35 us
    pallas_call x5, Pallas kernels, call(): pl.pallas_call(kernel, out_shape=out_shape, in_specs=[VMEM] * len(operand...  6.95 us
    pallas_call x1, Pallas kernels, per_device(): pl.pallas_call(functools.partial(pack, order), out_shape=jax.ShapeDtypeSt...  1.17 us
  transfers between devices with their start and end apart: 2, of which 0 were waited for; matrix products, arithmetic and copies ran while one was open for 0% of the time, Pallas kernels for 7%

profile of v7, /device:TPU:0, one launch (start us, length us, event | category | flops | bytes accessed | tf_op | source)
XLA Modules:
  0.0 29.5 jit_solution(5728891845544677821)
XLA Ops:
  0.0 0.0 copy-start
  0.0 0.0 copy-start.1
  0.0 0.0 slice-start
  0.0 0.0 slice-start.1
  0.0 1.2 %pack.1 = bf16[8,2,3584]{2,1,0:T(2,128)(2,1)S(1)} custom-call(s32[2,8]{1,0:T(2,128)} %bitcast.4, bf16[8,3584]{1,0:T(8,128)(2,1)} %rows_hbm.1), custom_call_target="tpu_custom_call" | custom-call | flops 19818086400 | tf_op jit(solution)/shard_map/pack/pallas_call | solution.py:159
  1.2 11.4 %all_to_all.10.refs_2_ = bf16[8,2,3584]{2,1,0:T(2,128)(2,1)S(1)} all-to-all(bf16[8,2,3584]{2,1,0:T(2,128)(2,1)S(1)} %pack.1), channel_id=1, replica_groups={{10,0,4,14,2,6,12,8},{11,1,5,15,3,7,13,9},{26,16,20,30,18,22,28,24},{27..., dimensions={0} | all-to-all | bytes 229376 | tf_op jit(solution)/shard_map/all_to_all | solution.py:181
  12.6 0.0 copy-done
  12.6 0.0 copy-done.1
  12.6 2.9 %project.2.gate_ref.refs_1_ = f32[3,16,1024]{2,1,0:T(8,128)S(1)} custom-call(bf16[3584,2048]{1,0:T(8,128)(2,1)S(1)} %copy-done, bf16[3584,2048]{1,0:T(8,128)(2,1)S(1)} %copy-done.1, bf16[8,2,3584]{2,1,0:T(2,128)(2,1)S(1)} %all_to_all.10.refs_2_), custom_call_target="tpu_custom_call" | custom-call | flops 352321536 | tf_op jit(solution)/shard_map/project/pallas_call | solution.py:29
  15.5 0.0 collective-permute-start
  15.6 0.0 slice-done
  15.6 0.0 slice-done.1
  15.6 0.0 slice-done.2
  15.6 0.0 slice-done.3
  15.6 1.1 %project.3.refs_1_ = f32[1,16,1024]{2,1,0:T(8,128)S(1)} custom-call(bf16[3584,2048]{1,0:T(8,128)(2,1)S(1)} %copy-done, bf16[2048,3584]{1,0:T(8,128)(2,1)S(1)} %bitcast.3, bf16[8,2,3584]{2,1,0:T(2,128)(2,1)S(1)} %all_to_all.10.refs_2_), custom_call_target="tpu_custom_call" | custom-call | flops 117440512 | tf_op jit(solution)/shard_map/project/pallas_call | solution.py:29
  16.7 0.5 %collective-permute-start.1 = (f32[1,16,1024]{2,1,0:T(8,128)S(1)}, f32[1,16,1024]{2,1,0:T(8,128)S(1)}, u32[]{:S(2)}, u32[]{:S(2)}) collective-permute-start(f32[1,16,1024]{2,1,0:T(8,128)S(1)} %project.3.refs_1_), channel_id=1, source_target_pairs={{0,1},{1,0},{2,3},{3,2},{4,5},{5,4},{6,7},{7,6},{8,9},{9,8},{10,11... | collective-permute-start | bytes 196616 | tf_op jit(solution)/shard_map/ppermute | solution.py:195
  17.2 0.0 collective-permute-done.refs_0_.refs_2_
  17.2 1.1 %down.2.refs_3_ = f32[16,3584]{1,0:T(8,128)S(1)} custom-call(f32[3,16,1024]{2,1,0:T(8,128)S(1)} %project.2.gate_ref.refs_1_, bf16[2048,3584]{1,0:T(8,128)(2,1)S(1)} %bitcast.3, f32[3,16,1024]{2,1,0:T(8,128)S(1)} %collective-permute-done.refs_0_.refs_2_, f32[3,16,1024]{2,1,0:T(8,128)S(1)} %project.2.gate_ref.refs_1_, ...), custom_call_target="tpu_custom_call" | custom-call | flops 117440512 | tf_op jit(solution)/shard_map/down/pallas_call | solution.py:29
  18.2 0.0 collective-permute-done.1.refs_2_
  18.2 0.0 copy-done.2
  18.2 0.0 copy-done.3
  18.2 1.1 %down.3 = (bf16[8,2,3584]{2,1,0:T(2,128)(2,1)S(1)}, bf16[24,16]{1,0:T(8,128)(2,1)S(1)}) custom-call(f32[3,16,1024]{2,1,0:T(8,128)S(1)} %project.2.gate_ref.refs_1_, bf16[2048,3584]{1,0:T(8,128)(2,1)S(1)} %bitcast.3, f32[3,16,1024]{2,1,0:T(8,128)S(1)} %collective-permute-done.refs_0_.refs_2_, f32[1,16,1024]{2,1,0:T(8,128)S(1)} %project.3.refs_1_, ...), custom_call_target="tpu_custom_call" | custom-call | flops 117440512 | tf_op jit(solution)/shard_map/down/pallas_call | solution.py:29
  19.3 9.3 %all_to_all.11.slots_ref = bf16[8,2,3584]{2,1,0:T(2,128)(2,1)S(1)} all-to-all(bf16[8,2,3584]{2,1,0:T(2,128)(2,1)S(1)} %get-tuple-element.8), channel_id=1, replica_groups={{10,0,4,14,2,6,12,8},{11,1,5,15,3,7,13,9},{26,16,20,30,18,22,28,24},{27..., dimensions={0} | all-to-all | bytes 229376 | tf_op jit(solution)/shard_map/all_to_all | solution.py:219
  28.7 0.8 %unpack.1 = bf16[8,3584]{1,0:T(8,128)(2,1)} custom-call(bf16[24,16]{1,0:T(8,128)(2,1)S(1)} %get-tuple-element.7.terms_ref, bf16[8,2,3584]{2,1,0:T(2,128)(2,1)S(1)} %all_to_all.11.slots_ref), custom_call_target="tpu_custom_call" | custom-call | tf_op jit(solution)/shard_map/unpack/pallas_call | solution.py:29
  (5 shorter events, 0.0 us)
Async XLA Ops:
  0.0 12.6 %copy-start = (bf16[3584,2048]{1,0:T(8,128)(2,1)S(1)}, bf16[3584,2048]{1,0:T(8,128)(2,1)}, u32[]{:S(2)}) copy-start(bf16[3584,2048]{1,0:T(8,128)(2,1)} %refs_0_.3) | copy-start | bytes 44040196
  0.0 12.6 %copy-start.1 = (bf16[3584,2048]{1,0:T(8,128)(2,1)S(1)}, bf16[3584,2048]{1,0:T(8,128)(2,1)}, u32[]{:S(2)}) copy-start(bf16[3584,2048]{1,0:T(8,128)(2,1)} %refs_1_.2) | copy-start | bytes 44040196
  0.0 15.5 %slice-start = ((s8[14680064]{0:T(1024)(128)(4,1)}), s8[4194304]{0:T(1024)(128)(4,1)S(1)}, s32[]{:S(2)}) async-start(s8[14680064]{0:T(1024)(128)(4,1)} %bitcast.2), calls=%async_computation.2 | async-start | bytes 8388608
  0.0 15.6 %slice-start.1 = ((s8[14680064]{0:T(1024)(128)(4,1)}), s8[4194304]{0:T(1024)(128)(4,1)S(1)}, s32[]{:S(2)}) async-start(s8[14680064]{0:T(1024)(128)(4,1)} %bitcast.2), calls=%async_computation.3 | async-start | bytes 8388608
  0.0 15.6 %slice-start.2 = ((s8[14680064]{0:T(1024)(128)(4,1)}), s8[4194304]{0:T(1024)(128)(4,1)S(1)}, s32[]{:S(2)}) async-start(s8[14680064]{0:T(1024)(128)(4,1)} %bitcast.2), calls=%async_computation.4 | async-start | bytes 8388608
  12.6 3.0 %slice-start.3 = ((s8[14680064]{0:T(1024)(128)(4,1)}), s8[2097152]{0:T(1024)(128)(4,1)S(1)}, s32[]{:S(2)}) async-start(s8[14680064]{0:T(1024)(128)(4,1)} %bitcast.2), calls=%async_computation.5 | async-start | bytes 4194304
  15.5 1.6 %collective-permute-start = (f32[3,16,1024]{2,1,0:T(8,128)S(1)}, f32[3,16,1024]{2,1,0:T(8,128)S(1)}, u32[]{:S(2)}, u32[]{:S(2)}) collective-permute-start(f32[3,16,1024]{2,1,0:T(8,128)S(1)} %project.2.gate_ref.refs_1_), channel_id=1, source_target_pairs={{0,1},{1,0},{2,3},{3,2},{4,5},{5,4},{6,7},{7,6},{8,9},{9,8},{10,11... | collective-permute-start | bytes 589832 | tf_op jit(solution)/shard_map/ppermute | solution.py:195
  16.7 1.6 %copy-start.2 = (s32[8,2]{0,1:T(2,128)S(1)}, s32[8,2]{0,1:T(2,128)}, u32[]{:S(2)}) copy-start(s32[8,2]{0,1:T(2,128)} %param.7) | copy-start | bytes 196
  16.7 1.6 %copy-start.3 = (f32[8,2]{0,1:T(2,128)S(1)}, f32[8,2]{0,1:T(2,128)}, u32[]{:S(2)}) copy-start(f32[8,2]{0,1:T(2,128)} %param.8) | copy-start | bytes 196
  16.7 1.6 %collective-permute-start.1 = (f32[1,16,1024]{2,1,0:T(8,128)S(1)}, f32[1,16,1024]{2,1,0:T(8,128)S(1)}, u32[]{:S(2)}, u32[]{:S(2)}) collective-permute-start(f32[1,16,1024]{2,1,0:T(8,128)S(1)} %project.3.refs_1_), channel_id=1, source_target_pairs={{0,1},{1,0},{2,3},{3,2},{4,5},{5,4},{6,7},{7,6},{8,9},{9,8},{10,11... | collective-permute-start | bytes 196616 | tf_op jit(solution)/shard_map/ppermute | solution.py:195
